TPU v7x, 512 devices: a whole 4x8x8 slice. The times are simulated.
512 devices in a mesh: xy: 64 (over z_lo, y, core), gz: 8 (over z_hi, x).
Axes of the slice: x: 4, y: 8, z: 8 (z_hi: 2, z_lo: 4; z = z_hi * 4 + z_lo), core: 2. Of those that a mesh axis runs over, the one named last changes fastest.
Arguments:
- e_check: float32 [3, 512, 16, 1024], P(None, 'xy', 'gz'), may hold values from -6 to 6
- h_check: float32 [3, 512, 16, 1024], P(None, 'xy', 'gz'), may hold values from -6 to 6
- adj_e: float32 [3, 512, 16, 1024], P(None, 'xy', 'gz'), may hold values from -6 to 6
- adj_h: float32 [3, 512, 16, 1024], P(None, 'xy', 'gz'), may hold values from -6 to 6
- material: int32 [512, 16, 1024], P('xy', 'gz'), may hold values from 0 to 3
- owner: int32 [512, 16, 1024], P('xy', 'gz'), may hold values from 0 to 7
- permittivity: float32 [4], replicated, may hold values from 1 to 4
Outputs:
- adj_e_out: float32 [3, 512, 16, 1024], P(None, 'xy', 'gz')
- adj_h_out: float32 [3, 512, 16, 1024], P(None, 'xy', 'gz')
- height_grad: float32 [8], replicated
All inputs are finite; a program needn't handle non-finite values.
Results may differ from a plain program's by a relative error of at most 0.0003.
Values sent between devices are 32-bit elements; how exact they have to be, the bound alone decides.
No kernel may reach another device: no remote copies, remote signals or barrier semaphores. Data moves between devices by JAX's collectives and lax.ppermute only.
A program may use at most 64 MiB of HBM per device.

v0:
```python
import functools

import jax
import jax.numpy as jnp
from jax import lax
from jax.sharding import Mesh
from jax.sharding import PartitionSpec as P

NI = 8
XY = ("xy_0", "xy_1", "xy_2")
GZ = ("gz_0", "gz_1")
XY_GZ = ("xy_0", "xy_1", "xy_2", "gz_0", "gz_1")


COURANT = 0.5


def shifted(value, axis, steps):
    count = lax.axis_size(axis)
    leading, last = (max(0, -steps), min(count, count - steps))
    return lax.ppermute(value, axis, [(source, source + steps) for source in range(leading, last)])


def one_axis_at_a_time(x, axes):
    return functools.reduce(lax.psum, axes, x)


def ahead_diff(values, edge_plane, dim_axis):
    dim_axis = values.ndim + dim_axis
    count = values.shape[dim_axis]
    later = jnp.concatenate(
        [lax.slice_in_dim(values, 1, count, axis=dim_axis), edge_plane], axis=dim_axis
    )
    return later - values


def behind_diff(values, edge_plane, dim_axis):
    dim_axis = values.ndim + dim_axis
    count = values.shape[dim_axis]
    earlier = jnp.concatenate(
        [edge_plane, lax.slice_in_dim(values, 0, count - 1, axis=dim_axis)], axis=dim_axis
    )
    return values - earlier


def curl_fwd(fields):
    above_x = shifted(fields[..., 1:3, :1, :, :], XY, -1)
    above_z = shifted(fields[..., 0:2, :, :1, :], GZ, -1)
    comp_x = fields[..., 0, :, :, :]
    comp_y = fields[..., 1, :, :, :]
    comp_z = fields[..., 2, :, :, :]
    zero_y = jnp.zeros_like(comp_x[..., :1])
    curl_x = ahead_diff(comp_z, zero_y, -1) - ahead_diff(comp_y, above_z[..., 1, :, :, :], -2)
    curl_y = ahead_diff(comp_x, above_z[..., 0, :, :, :], -2) - ahead_diff(
        comp_z, above_x[..., 1, :, :, :], -3
    )
    curl_z = ahead_diff(comp_y, above_x[..., 0, :, :, :], -3) - ahead_diff(comp_x, zero_y, -1)
    return jnp.stack([curl_x, curl_y, curl_z], axis=-4)


def curl_bwd(fields):
    below_x = shifted(fields[..., 1:3, -1:, :, :], XY, 1)
    below_z = shifted(fields[..., 0:2, :, -1:, :], GZ, 1)
    comp_x = fields[..., 0, :, :, :]
    comp_y = fields[..., 1, :, :, :]
    comp_z = fields[..., 2, :, :, :]
    zero_y = jnp.zeros_like(comp_x[..., :1])
    curl_x = behind_diff(comp_z, zero_y, -1) - behind_diff(comp_y, below_z[..., 1, :, :, :], -2)
    curl_y = behind_diff(comp_x, below_z[..., 0, :, :, :], -2) - behind_diff(
        comp_z, below_x[..., 1, :, :, :], -3
    )
    curl_z = behind_diff(comp_y, below_x[..., 0, :, :, :], -3) - behind_diff(comp_x, zero_y, -1)
    return jnp.stack([curl_x, curl_y, curl_z], axis=-4)


def interface_sums(weight, owner):
    onehot = (owner.reshape(-1, 1) == jnp.arange(NI, dtype=jnp.int32)[None, :]).astype(jnp.float32)
    return jnp.dot(weight.reshape(1, -1), onehot, precision=lax.Precision.HIGHEST)[0]


def body(e_check, h_check, adj_e, adj_h, material, owner, permittivity):
    e_coef = jnp.zeros(material.shape, jnp.float32)
    for kind_index in range(4):
        e_coef = e_coef + jnp.where(material == kind_index, COURANT / permittivity[kind_index], 0.0)
    electric = [e_check]
    magnetic = h_check
    adjoint_e = [adj_e]
    adjoint_h = adj_h
    for index_step in range(2):
        first = curl_fwd(jnp.stack([electric[-1], e_coef * adjoint_e[-1]], axis=0))
        magnetic = magnetic - COURANT * first[0]
        adjoint_h = adjoint_h + first[1]
        second = curl_bwd(jnp.stack([magnetic, adjoint_h], axis=0))
        electric.append(electric[-1] + e_coef * second[0])
        adjoint_e.append(adjoint_e[-1] - COURANT * second[1])
    partials = []
    for later_step in (2, 1):
        adjoint_now = adjoint_e[2 - later_step]
        weight = e_coef * jnp.sum(
            adjoint_now * (electric[later_step] - electric[later_step - 1]), axis=0
        )
        partials.append(interface_sums(weight, owner))
    gradient = jnp.zeros((NI,), jnp.float32)
    for partial_sum in partials:
        gradient = gradient + one_axis_at_a_time(partial_sum, XY_GZ)
    total_cells = (
        e_check.shape[1]
        * lax.axis_size(XY)
        * e_check.shape[2]
        * lax.axis_size(GZ)
        * e_check.shape[3]
    )
    gradient = gradient / jnp.sqrt(jnp.float32(total_cells / NI))
    return (adjoint_e[-1], adjoint_h, gradient)


def solution(mesh):
    split = Mesh(mesh.devices.reshape(4, 8, 2, 2, 4), ("xy_0", "xy_1", "xy_2", "gz_0", "gz_1"))
    return jax.shard_map(
        body,
        mesh=split,
        in_specs=(
            P(None, XY, GZ, None),
            P(None, XY, GZ, None),
            P(None, XY, GZ, None),
            P(None, XY, GZ, None),
            P(XY, GZ, None),
            P(XY, GZ, None),
            P(),
        ),
        out_specs=(P(None, XY, GZ, None), P(None, XY, GZ, None), P()),
        check_vma=False,
    )
```

profile of v0, /device:TPU:1, one launch (start us, length us, event | category | flops | bytes accessed | tf_op | source)
XLA Modules:
  0.0 120.9 jit_solution(12816583631142692217)
XLA Ops:
  0.6 1.5 %fusion.70 = (f32[1]{0:T(128)}, f32[1]{0:T(128)}, f32[1]{0:T(128)}, f32[1]{0:T(128)}) fusion(f32[4]{0:T(128)} %param.13), kind=kLoop, calls=%fused_computation.166 | loop fusion | bytes 32 | tf_op jit(solution)/shard_map/slice | solution.py:84
  4.9 0.9 fusion.65
  5.8 1.0 multiply_bitcast_fusion.1
  6.9 0.1 fusion.22
  7.0 1.3 %collective-permute-start = (f32[2,2,8,1,1024]{4,3,2,1,0:T(1,128)S(1)}, f32[2,2,8,1,1024]{4,3,2,1,0:T(1,128)S(1)}, u32[]{:S(2)}, u32[]{:S(2)}) collective-permute-start(f32[2,2,8,1,1024]{4,3,2,1,0:T(1,128)S(1)} %fusion.22), channel_id=1, source_target_pairs={{1,0},{2,1},{3,2},{4,3},{5,4},{6,5},{7,6},{9,8},{10,9},{11,10},{12... | collective-permute-start | bytes 393224 | tf_op jit(solution)/shard_map/ppermute | solution.py:21
  8.4 8.8 %collective-permute-start.1 = (f32[2,2,1,2,1024]{4,3,2,1,0:T(2,128)S(1)}, f32[2,2,1,2,1024]{4,3,2,1,0:T(2,128)S(1)}, u32[]{:S(2)}, u32[]{:S(2)}) collective-permute-start(f32[2,2,1,2,1024]{4,3,2,1,0:T(2,128)S(1)} %pad_maximum_fusion.7), channel_id=1, source_target_pairs={{8,0},{16,8},{24,16},{32,24},{40,32},{48,40},{56,48},{64,56},{72,6... | collective-permute-start | bytes 98312 | tf_op jit(solution)/shard_map/ppermute | solution.py:21
  17.2 0.2 fusion.33
  17.4 0.1 slice_bitcast_fusion.14
  17.4 0.2 slice.290
  17.6 0.2 slice.305
  17.9 0.1 slice.293
  18.0 0.8 copy-done.6
  18.8 0.2 fusion.37
  19.0 0.3 fusion.36
  19.4 0.0 copy-start.3
  19.4 0.2 pad_maximum_fusion
  19.6 0.7 copy-done.3
  20.3 0.1 copy-done.4
  20.4 0.2 fusion.67
  20.6 0.2 fusion.30
  20.9 1.9 %collective-permute-start.3 = (f32[2,2,1,2,1024]{4,3,2,1,0:T(2,128)S(1)}, f32[2,2,1,2,1024]{4,3,2,1,0:T(2,128)S(1)}, u32[]{:S(2)}, u32[]{:S(2)}) collective-permute-start(f32[2,2,1,2,1024]{4,3,2,1,0:T(2,128)S(1)} %pad_maximum_fusion.6), channel_id=1, source_target_pairs={{0,8},{8,16},{16,24},{24,32},{32,40},{40,48},{48,56},{56,64},{64,7... | collective-permute-start | bytes 98312 | tf_op jit(solution)/shard_map/ppermute | solution.py:21
  22.9 0.2 fusion.21
  23.1 4.3 %collective-permute-start.2 = (f32[2,2,8,1,1024]{4,3,2,1,0:T(1,128)S(1)}, f32[2,2,8,1,1024]{4,3,2,1,0:T(1,128)S(1)}, u32[]{:S(2)}, u32[]{:S(2)}) collective-permute-start(f32[2,2,8,1,1024]{4,3,2,1,0:T(1,128)S(1)} %fusion.21), channel_id=1, source_target_pairs={{0,1},{1,2},{2,3},{3,4},{4,5},{5,6},{6,7},{8,9},{9,10},{10,11},{11... | collective-permute-start | bytes 393224 | tf_op jit(solution)/shard_map/ppermute | solution.py:21
  27.4 2.3 %collective-permute-done.2 = f32[2,2,8,1,1024]{4,3,2,1,0:T(1,128)S(1)} collective-permute-done((f32[2,2,8,1,1024]{4,3,2,1,0:T(1,128)S(1)}, f32[2,2,8,1,1024]{4,3,2,1,0:T(1,128)S(1)}, u32[]{:S(2)}, u32[]{:S(2)}) %collective-permute-start.2) | collective-permute-done | bytes 131104 | tf_op jit(solution)/shard_map/ppermute | solution.py:21
  29.7 0.2 fusion.43
  30.0 0.5 fusion.42
  30.5 0.0 copy-start.2
  30.5 0.2 pad_maximum_fusion.1
  30.7 0.7 copy-done.2
  31.4 0.3 fusion.68
  31.7 0.2 fusion.27
  31.9 3.3 %collective-permute-start.5 = (f32[2,2,1,2,1024]{4,3,2,1,0:T(2,128)S(1)}, f32[2,2,1,2,1024]{4,3,2,1,0:T(2,128)S(1)}, u32[]{:S(2)}, u32[]{:S(2)}) collective-permute-start(f32[2,2,1,2,1024]{4,3,2,1,0:T(2,128)S(1)} %pad_maximum_fusion.5), channel_id=1, source_target_pairs={{8,0},{16,8},{24,16},{32,24},{40,32},{48,40},{56,48},{64,56},{72,6... | collective-permute-start | bytes 98312 | tf_op jit(solution)/shard_map/ppermute | solution.py:21
  35.1 0.1 slice_bitcast_fusion.10
  35.2 0.1 fusion.20
  35.4 0.2 slice.330
  35.6 0.2 slice.345
  35.8 0.1 slice.333
  35.9 1.3 %collective-permute-start.4 = (f32[2,2,8,1,1024]{4,3,2,1,0:T(1,128)S(1)}, f32[2,2,8,1,1024]{4,3,2,1,0:T(1,128)S(1)}, u32[]{:S(2)}, u32[]{:S(2)}) collective-permute-start(f32[2,2,8,1,1024]{4,3,2,1,0:T(1,128)S(1)} %fusion.20), channel_id=1, source_target_pairs={{1,0},{2,1},{3,2},{4,3},{5,4},{6,5},{7,6},{9,8},{10,9},{11,10},{12... | collective-permute-start | bytes 393224 | tf_op jit(solution)/shard_map/ppermute | solution.py:21
  37.2 6.1 %collective-permute-done.4 = f32[2,2,8,1,1024]{4,3,2,1,0:T(1,128)S(1)} collective-permute-done((f32[2,2,8,1,1024]{4,3,2,1,0:T(1,128)S(1)}, f32[2,2,8,1,1024]{4,3,2,1,0:T(1,128)S(1)}, u32[]{:S(2)}, u32[]{:S(2)}) %collective-permute-start.4) | collective-permute-done | bytes 131104 | tf_op jit(solution)/shard_map/ppermute | solution.py:21
  43.3 0.2 fusion.49
  43.5 0.3 fusion.48
  43.9 0.2 pad_maximum_fusion.2
  44.0 0.3 fusion.10
  44.4 0.0 copy-start.1
  44.4 0.2 fusion.24
  44.6 2.2 %collective-permute-start.7 = (f32[2,2,1,2,1024]{4,3,2,1,0:T(2,128)S(1)}, f32[2,2,1,2,1024]{4,3,2,1,0:T(2,128)S(1)}, u32[]{:S(2)}, u32[]{:S(2)}) collective-permute-start(f32[2,2,1,2,1024]{4,3,2,1,0:T(2,128)S(1)} %pad_maximum_fusion.4), channel_id=1, source_target_pairs={{0,8},{8,16},{16,24},{24,32},{32,40},{40,48},{48,56},{56,64},{64,7... | collective-permute-start | bytes 98312 | tf_op jit(solution)/shard_map/ppermute | solution.py:21
  46.9 0.2 fusion.19
  47.2 6.9 %collective-permute-start.6 = (f32[2,2,8,1,1024]{4,3,2,1,0:T(1,128)S(1)}, f32[2,2,8,1,1024]{4,3,2,1,0:T(1,128)S(1)}, u32[]{:S(2)}, u32[]{:S(2)}) collective-permute-start(f32[2,2,8,1,1024]{4,3,2,1,0:T(1,128)S(1)} %fusion.19), channel_id=1, source_target_pairs={{0,1},{1,2},{2,3},{3,4},{4,5},{5,6},{6,7},{8,9},{9,10},{10,11},{11... | collective-permute-start | bytes 393224 | tf_op jit(solution)/shard_map/ppermute | solution.py:21
  54.1 1.9 %collective-permute-done.6 = f32[2,2,8,1,1024]{4,3,2,1,0:T(1,128)S(1)} collective-permute-done((f32[2,2,8,1,1024]{4,3,2,1,0:T(1,128)S(1)}, f32[2,2,8,1,1024]{4,3,2,1,0:T(1,128)S(1)}, u32[]{:S(2)}, u32[]{:S(2)}) %collective-permute-start.6) | collective-permute-done | bytes 131104 | tf_op jit(solution)/shard_map/ppermute | solution.py:21
  56.0 0.2 fusion.55
  56.3 0.5 fusion.54
  56.8 0.2 pad_maximum_fusion.3
  57.0 1.2 fusion.18
  58.2 0.1 fusion.69
  58.3 0.1 reshape.68
  58.4 0.1 reshape.66
  58.5 0.7 convolution_bitcast_fusion
  59.2 0.7 fusion
  59.9 11.5 %psum.84 = f32[8]{0:T(128)S(1)} all-reduce(f32[8]{0:T(128)S(1)} %fusion), channel_id=1, replica_groups=mesh['xy_0'=4,'xy_1'=8,'xy_2'=2,'gz_0'=2,'gz_1'=4] {'xy_0'}, use_global_device_ids=true, to_apply=%region_1.2 | all-reduce | flops 8 | bytes 64 | tf_op jit(solution)/shard_map/psum | solution.py:25
  71.4 13.4 %psum.83 = f32[8]{0:T(128)S(1)} all-reduce(f32[8]{0:T(128)S(1)} %psum.84), channel_id=1, replica_groups=mesh['xy_0'=4,'xy_1'=8,'xy_2'=2,'gz_0'=2,'gz_1'=4] {'xy_1'}, use_global_device_ids=true, to_apply=%region_2.3 | all-reduce | flops 8 | bytes 64 | tf_op jit(solution)/shard_map/psum | solution.py:25
  84.8 8.4 %psum.82 = f32[8]{0:T(128)S(1)} all-reduce(f32[8]{0:T(128)S(1)} %psum.83), channel_id=1, replica_groups=mesh['xy_0'=4,'xy_1'=8,'xy_2'=2,'gz_0'=2,'gz_1'=4] {'xy_2'}, use_global_device_ids=true, to_apply=%region_3.4 | all-reduce | flops 8 | bytes 64 | tf_op jit(solution)/shard_map/psum | solution.py:25
  93.3 20.5 %psum.81 = f32[8]{0:T(128)S(1)} all-reduce(f32[8]{0:T(128)S(1)} %psum.82), channel_id=1, replica_groups=mesh['xy_0'=4,'xy_1'=8,'xy_2'=2,'gz_0'=2,'gz_1'=4] {'gz_0'}, use_global_device_ids=true, to_apply=%region_4.5 | all-reduce | flops 8 | bytes 64 | tf_op jit(solution)/shard_map/psum | solution.py:25
  113.8 6.6 %psum.80 = f32[8]{0:T(128)S(1)} all-reduce(f32[8]{0:T(128)S(1)} %psum.81), channel_id=1, replica_groups=mesh['xy_0'=4,'xy_1'=8,'xy_2'=2,'gz_0'=2,'gz_1'=4] {'gz_1'}, use_global_device_ids=true, to_apply=%region_5.6 | all-reduce | flops 8 | bytes 64 | tf_op jit(solution)/shard_map/psum | solution.py:25
  120.3 0.5 broadcast_multiply_fusion
  (37 shorter events, 0.4 us)
Async XLA Ops:
  5.8 1.1 copy-start
  7.0 11.8 %collective-permute-start = (f32[2,2,8,1,1024]{4,3,2,1,0:T(1,128)S(1)}, f32[2,2,8,1,1024]{4,3,2,1,0:T(1,128)S(1)}, u32[]{:S(2)}, u32[]{:S(2)}) collective-permute-start(f32[2,2,8,1,1024]{4,3,2,1,0:T(1,128)S(1)} %fusion.22), channel_id=1, source_target_pairs={{1,0},{2,1},{3,2},{4,3},{5,4},{6,5},{7,6},{9,8},{10,9},{11,10},{12... | collective-permute-start | bytes 393224 | tf_op jit(solution)/shard_map/ppermute | solution.py:21
  8.4 10.4 %collective-permute-start.1 = (f32[2,2,1,2,1024]{4,3,2,1,0:T(2,128)S(1)}, f32[2,2,1,2,1024]{4,3,2,1,0:T(2,128)S(1)}, u32[]{:S(2)}, u32[]{:S(2)}) collective-permute-start(f32[2,2,1,2,1024]{4,3,2,1,0:T(2,128)S(1)} %pad_maximum_fusion.7), channel_id=1, source_target_pairs={{8,0},{16,8},{24,16},{32,24},{40,32},{48,40},{56,48},{64,56},{72,6... | collective-permute-start | bytes 98312 | tf_op jit(solution)/shard_map/ppermute | solution.py:21
  17.9 0.8 copy-start.6
  19.4 0.9 copy-start.3
  19.4 1.0 copy-start.4
  20.9 6.5 %collective-permute-start.3 = (f32[2,2,1,2,1024]{4,3,2,1,0:T(2,128)S(1)}, f32[2,2,1,2,1024]{4,3,2,1,0:T(2,128)S(1)}, u32[]{:S(2)}, u32[]{:S(2)}) collective-permute-start(f32[2,2,1,2,1024]{4,3,2,1,0:T(2,128)S(1)} %pad_maximum_fusion.6), channel_id=1, source_target_pairs={{0,8},{8,16},{16,24},{24,32},{32,40},{40,48},{48,56},{56,64},{64,7... | collective-permute-start | bytes 98312 | tf_op jit(solution)/shard_map/ppermute | solution.py:21
  23.1 6.6 %collective-permute-start.2 = (f32[2,2,8,1,1024]{4,3,2,1,0:T(1,128)S(1)}, f32[2,2,8,1,1024]{4,3,2,1,0:T(1,128)S(1)}, u32[]{:S(2)}, u32[]{:S(2)}) collective-permute-start(f32[2,2,8,1,1024]{4,3,2,1,0:T(1,128)S(1)} %fusion.21), channel_id=1, source_target_pairs={{0,1},{1,2},{2,3},{3,4},{4,5},{5,6},{6,7},{8,9},{9,10},{10,11},{11... | collective-permute-start | bytes 393224 | tf_op jit(solution)/shard_map/ppermute | solution.py:21
  30.5 0.9 copy-start.2
  31.9 5.3 %collective-permute-start.5 = (f32[2,2,1,2,1024]{4,3,2,1,0:T(2,128)S(1)}, f32[2,2,1,2,1024]{4,3,2,1,0:T(2,128)S(1)}, u32[]{:S(2)}, u32[]{:S(2)}) collective-permute-start(f32[2,2,1,2,1024]{4,3,2,1,0:T(2,128)S(1)} %pad_maximum_fusion.5), channel_id=1, source_target_pairs={{8,0},{16,8},{24,16},{32,24},{40,32},{48,40},{56,48},{64,56},{72,6... | collective-permute-start | bytes 98312 | tf_op jit(solution)/shard_map/ppermute | solution.py:21
  35.9 7.4 %collective-permute-start.4 = (f32[2,2,8,1,1024]{4,3,2,1,0:T(1,128)S(1)}, f32[2,2,8,1,1024]{4,3,2,1,0:T(1,128)S(1)}, u32[]{:S(2)}, u32[]{:S(2)}) collective-permute-start(f32[2,2,8,1,1024]{4,3,2,1,0:T(1,128)S(1)} %fusion.20), channel_id=1, source_target_pairs={{1,0},{2,1},{3,2},{4,3},{5,4},{6,5},{7,6},{9,8},{10,9},{11,10},{12... | collective-permute-start | bytes 393224 | tf_op jit(solution)/shard_map/ppermute | solution.py:21
  44.4 2.5 %copy-start.1 = (f32[3,8,2,1024]{3,2,1,0:T(2,128)}, f32[3,8,2,1024]{3,2,1,0:T(2,128)S(1)}, u32[]{:S(2)}) copy-start(f32[3,8,2,1024]{3,2,1,0:T(2,128)S(1)} %get-tuple-element.7) | copy-start | bytes 589828
  44.6 9.5 %collective-permute-start.7 = (f32[2,2,1,2,1024]{4,3,2,1,0:T(2,128)S(1)}, f32[2,2,1,2,1024]{4,3,2,1,0:T(2,128)S(1)}, u32[]{:S(2)}, u32[]{:S(2)}) collective-permute-start(f32[2,2,1,2,1024]{4,3,2,1,0:T(2,128)S(1)} %pad_maximum_fusion.4), channel_id=1, source_target_pairs={{0,8},{8,16},{16,24},{24,32},{32,40},{40,48},{48,56},{56,64},{64,7... | collective-permute-start | bytes 98312 | tf_op jit(solution)/shard_map/ppermute | solution.py:21
  47.2 8.8 %collective-permute-start.6 = (f32[2,2,8,1,1024]{4,3,2,1,0:T(1,128)S(1)}, f32[2,2,8,1,1024]{4,3,2,1,0:T(1,128)S(1)}, u32[]{:S(2)}, u32[]{:S(2)}) collective-permute-start(f32[2,2,8,1,1024]{4,3,2,1,0:T(1,128)S(1)} %fusion.19), channel_id=1, source_target_pairs={{0,1},{1,2},{2,3},{3,4},{4,5},{5,6},{6,7},{8,9},{9,10},{10,11},{11... | collective-permute-start | bytes 393224 | tf_op jit(solution)/shard_map/ppermute | solution.py:21
  57.0 1.2 copy-start.5
where the time goes:
time: 123 us; the launch traced here: 121 us
  blocking collectives  60.4 us (49%)
  starting transfers between devices  29.9 us (24%)
  waiting for transfers between devices  10.3 us (8%)
  other arithmetic  9.33 us (8%)
  local copies, waits for them, and re-layouts  5.44 us (4%)
  between operations  4 us (3%)
  matrix products  1.4 us (1%)
    psum x5, blocking collectives, one_axis_at_a_time(): return functools.reduce(lax.psum, axes, x)  60.4 us
    ppermute x8, starting transfers between devices, shifted(): lax.ppermute(value, axis, [(source, source + steps) for source in range(l...  29.9 us
    ppermute x8, waiting for transfers between devices, shifted(): lax.ppermute(value, axis, [(source, source + steps) for source in range(l...  10.3 us
  transfers between devices with their start and end apart: 8, of which 3 were waited for; matrix products, arithmetic and copies ran while one was open for 2% of the time, Pallas kernels for 0%

commit v1 on v0

v1 whole, which is shorter than its diff:
```python
import functools

import jax
import jax.numpy as jnp
from jax import lax
from jax.experimental import pallas as pl
from jax.experimental.pallas import tpu as pltpu
from jax.sharding import Mesh
from jax.sharding import PartitionSpec as P

NI = 8
AXES = ("zl", "y", "c", "zh", "x")
XY = ("zl", "y", "c")
GZ = ("zh", "x")
COURANT = 0.5
ALPHA = (-COURANT, 1.0)
BETA = (1.0, -COURANT)

UP_LINES = (("ax", 10), ("ay", 10), ("px", 8), ("py", 8))
DOWN_LINES = (("sx", 11), ("sy", 10), ("qx", 9), ("qy", 8))
LINES = 2 * 38 + 9
HALO = 26


def shift_later(u):
    lane = lax.broadcasted_iota(jnp.int32, u.shape, u.ndim - 1)
    row = lax.broadcasted_iota(jnp.int32, u.shape, u.ndim - 2)
    turned = pltpu.roll(u, 127, u.ndim - 1)
    carried = pltpu.roll(turned, 7, u.ndim - 2)
    return jnp.where(lane < 127, turned, jnp.where(row < 7, carried, 0.0))


def shift_earlier(u):
    lane = lax.broadcasted_iota(jnp.int32, u.shape, u.ndim - 1)
    row = lax.broadcasted_iota(jnp.int32, u.shape, u.ndim - 2)
    turned = pltpu.roll(u, 1, u.ndim - 1)
    carried = pltpu.roll(turned, 1, u.ndim - 2)
    return jnp.where(lane > 0, turned, jnp.where(row > 0, carried, 0.0))


def ahead_y(u):
    return shift_later(u) - u


def behind_y(u):
    return u - shift_earlier(u)


def table(material, values):
    out = jnp.zeros(material.shape, jnp.float32)
    for kind in range(4):
        out = out + jnp.where(material == kind, values[kind], 0.0)
    return out


def coefs(eps_ref):
    return [COURANT / eps_ref[kind] for kind in range(4)]


def plane(z):
    return pl.ds(z, 8, stride=2)


def keep_low(u, count, flag):
    return jnp.concatenate([u[:count] * flag, u[count:]], axis=0)


def low_flag(axes):
    first = functools.reduce(jnp.logical_and, [lax.axis_index(a) == 0 for a in axes])
    return jnp.where(first, 0.0, 1.0).astype(jnp.float32)


def pack_kernel(eps_ref, e0, e1, h0, h1, g0, g1, k0, k1, m0, m1, pair_ref, next_ref):
    even = lax.axis_index("c") == 0
    values = coefs(eps_ref)

    def put(row, first, last):
        pair_ref[row] = jnp.where(even, last, first)
        next_ref[row] = jnp.where(even, first, last)

    for field, (first, last) in enumerate(((e0, e1), (h0, h1), (g0, g1), (k0, k1))):
        for comp in range(3):
            for k in range(2):
                put(field * 6 + comp * 2 + k, first[comp, k], last[comp, k])
    for k in range(2):
        put(24 + k, table(m0[k], values), table(m1[k], values))


def local_kernel(eps_ref, e, h, g, kf, m, pair_ref, next_ref, pay0, pay1, t1s, s1s, s0s, cs):
    even_x = lax.axis_index("c") == 0
    even_z = lax.axis_index("x") % 2 == 0
    x_flag = low_flag(XY)
    values = coefs(eps_ref)

    def below(row, z):
        return jnp.where(even_x, next_ref[row, plane(z), :], pair_ref[row, plane(z), :])[None]

    def above(row, z):
        return jnp.where(even_x, pair_ref[row, plane(z), :], next_ref[row, plane(z), :])[None]

    def extended(ref, base, comp, z):
        row = base + comp * 2
        return jnp.concatenate(
            [below(row, z), below(row + 1, z), ref[comp, :, plane(z), :], above(row, z), above(row + 1, z)],
            axis=0,
        )

    coef = []
    for z in range(2):
        own = table(m[:, plane(z), :], values)
        coef.append(jnp.concatenate([below(24, z), below(25, z), own, above(24, z), above(25, z)], axis=0))
        cs[z] = coef[z][1:11]

    def put(row, up, down):
        pay0[row] = jnp.where(even_z, up, down)
        pay1[row] = jnp.where(even_z, down, up)

    for chain in range(2):
        alpha, beta = ALPHA[chain], BETA[chain]
        if chain == 0:
            s = [[extended(e, 0, comp, z) for z in range(2)] for comp in range(3)]
            t = [[extended(h, 6, comp, z)[:11] for z in range(2)] for comp in range(3)]
        else:
            s = [[extended(g, 12, comp, z) * coef[z] for z in range(2)] for comp in range(3)]
            t = [[extended(kf, 18, comp, z)[:11] for z in range(2)] for comp in range(3)]
        sx, sy, sz = s
        t1 = [[None, None] for _ in range(3)]
        for z in range(2):
            dz_y = (sy[1] - sy[0])[:11] if z == 0 else -sy[1][:11]
            dz_x = (sx[1] - sx[0])[:11] if z == 0 else -sx[1][:11]
            t1[0][z] = t[0][z] + alpha * (ahead_y(sz[z][:11]) - dz_y)
            t1[1][z] = t[1][z] + alpha * (dz_x - (sz[z][1:] - sz[z][:11]))
            t1[2][z] = t[2][z] + alpha * ((sy[z][1:] - sy[z][:11]) - ahead_y(sx[z][:11]))
            for comp in range(3):
                t1[comp][z] = keep_low(t1[comp][z], 2, x_flag)
                t1s[chain, comp, z] = t1[comp][z]
        s1 = [[None, None] for _ in range(3)]
        for z in range(2):
            tx, ty, tz = t1[0][z], t1[1][z], t1[2][z]
            b = beta * coef[z][1:11]
            dz_y = ty[1:] if z == 0 else (ty - t1[1][0])[1:]
            dz_x = tx[1:] if z == 0 else (tx - t1[0][0])[1:]
            s1[0][z] = sx[z][1:11] + b * (behind_y(tz[1:]) - dz_y)
            s1[1][z] = sy[z][1:11] + b * (dz_x - (tz[1:] - tz[:10]))
            s1[2][z] = sz[z][1:11] + b * ((ty[1:] - ty[:10]) - behind_y(tx[1:]))
            for comp in range(3):
                s1s[chain, comp, z] = s1[comp][z]
        s0s[chain, 0] = sx[0][1:11]
        s0s[chain, 1] = sy[0][1:11]
        ax, ay = t1[0][1][1:], t1[1][1][1:]
        px = ax[1:9] + alpha * (ahead_y(s1[2][1][1:9]) + s1[1][1][1:9])
        py = ay[1:9] - alpha * (s1[0][1][1:9] + (s1[2][1][2:10] - s1[2][1][1:9]))
        up = jnp.concatenate([ax, ay, px, py, jnp.zeros((2, 8, 128), jnp.float32)], axis=0)
        down = jnp.concatenate([sx[0][:11], sy[0][1:11], s1[0][0][:9], s1[1][0][1:9]], axis=0)
        put(pl.ds(38 * chain, 38), up, down)
    put(pl.ds(76, 9), coef[1][2:11], coef[0][1:10])


def final_kernel(eps_ref, e, g, m, owner, r0, r1, t1s, s1s, s0s, cs, adj_e, adj_h, sums):
    even_z = lax.axis_index("x") % 2 == 0
    x_flag, z_flag = low_flag(XY), low_flag(GZ)
    values = coefs(eps_ref)
    inverse = [2.0 * eps_ref[kind] for kind in range(4)]

    def above(start, count):
        return jnp.where(even_z, r0[pl.ds(start, count)], r1[pl.ds(start, count)])

    def below(start, count):
        return jnp.where(even_z, r1[pl.ds(start, count)], r0[pl.ds(start, count)])

    c_up, c_low = above(76, 9), below(76, 9)
    own = slice(1, 9)
    kept = []
    for chain in range(2):
        alpha, beta = ALPHA[chain], BETA[chain]
        base = 38 * chain
        sx2, sy2, qx, qy = above(base, 11), above(base + 11, 10), above(base + 21, 9), above(base + 30, 8)
        ax, ay, px, py = below(base, 10), below(base + 10, 10), below(base + 20, 8), below(base + 28, 8)
        sx0, sy0 = s0s[chain, 0], s0s[chain, 1]
        tx = [t1s[chain, 0, 0][1:], t1s[chain, 0, 1][1:] - alpha * sy2]
        ty = [t1s[chain, 1, 0][1:], t1s[chain, 1, 1][1:] + alpha * sx2[1:]]
        tz = [t1s[chain, 2, 0][1:], t1s[chain, 2, 1][1:]]
        tx_low = (ax - alpha * sy0) * z_flag
        ty_low = (ay + alpha * sx0) * z_flag
        b0, b1 = beta * cs[0], beta * cs[1]
        div2 = (sx2[1:] - sx2[:10]) + behind_y(sy2)
        sx = [s1s[chain, 0, 0] + b0 * ty_low, s1s[chain, 0, 1] - alpha * b1 * sx2[1:]]
        sy = [s1s[chain, 1, 0] - b0 * tx_low, s1s[chain, 1, 1] - alpha * b1 * sy2]
        sz = [s1s[chain, 2, 0], s1s[chain, 2, 1] + alpha * b1 * div2]
        b_up, b_low = beta * c_up, beta * c_low
        sx.append(qx + b_up * ty[1][:9])
        sy_top = qy - b_up[1:] * tx[1][own]
        t2x, t2y, t2z = [], [], []
        for z in range(2):
            dz_y = (sy[1] - sy[0])[own] if z == 0 else sy_top - sy[1][own]
            dz_x = sx[z + 1][:9] - sx[z][:9]
            t2x.append(tx[z][own] + alpha * (ahead_y(sz[z][own]) - dz_y))
            y_new = ty[z][:9] + alpha * (dz_x - (sz[z][1:] - sz[z][:9]))
            z_new = tz[z][:9] + alpha * ((sy[z][1:] - sy[z][:9]) - ahead_y(sx[z][:9]))
            t2y.append(keep_low(y_new, 1, x_flag))
            t2z.append(keep_low(z_new, 1, x_flag))
        div0 = b_low * ((sx0[1:] - sx0[:9]) + behind_y(sy0[1:]))
        x_low = px - alpha * (sy0[own] + sy[0][own]) + alpha * alpha * (ahead_y(div0[:8]) - b_low[:8] * sy0[own])
        y_low = py + alpha * (sx0[own] + sx[0][own]) + alpha * alpha * (b_low[:8] * sx0[own] - (div0[1:] - div0[:8]))
        x_low, y_low = x_low * z_flag, y_low * z_flag
        curl = []
        for z in range(2):
            dz_y = t2y[z][1:] - (y_low if z == 0 else t2y[0][1:])
            dz_x = t2x[z] - (x_low if z == 0 else t2x[0])
            curl.append((
                behind_y(t2z[z][1:]) - dz_y,
                dz_x - (t2z[z][1:] - t2z[z][:8]),
                (t2y[z][1:] - t2y[z][:8]) - behind_y(t2x[z]),
            ))
        kept.append(([[s[z][own] for s in (sx, sy, sz)] for z in range(2)], curl))
        if chain == 1:
            for z in range(2):
                scale = table(m[:, plane(z), :], inverse)
                for comp, t2 in enumerate((t2x[z], t2y[z][1:], t2z[z][1:])):
                    adj_e[comp, :, plane(z), :] = kept[1][0][z][comp] * scale - COURANT * curl[z][comp]
                    adj_h[comp, :, plane(z), :] = t2

    totals = [jnp.zeros((8, 128), jnp.float32) for _ in range(NI)]
    for z in range(2):
        coef = table(m[:, plane(z), :], values)
        weight = jnp.zeros((8, 8, 128), jnp.float32)
        for comp in range(3):
            step = kept[0][0][z][comp] - e[comp, :, plane(z), :]
            weight = weight + kept[1][0][z][comp] * step
            weight = weight + coef * g[comp, :, plane(z), :] * (coef * kept[0][1][z][comp])
        who = owner[:, plane(z), :]
        for j in range(NI):
            totals[j] = totals[j] + jnp.sum(jnp.where(who == j, weight, 0.0), axis=0)
    lane = lax.broadcasted_iota(jnp.int32, (1, 128), 1)
    row = jnp.zeros((1, 128), jnp.float32)
    for j in range(NI):
        row = row + jnp.where(lane == j, jnp.sum(totals[j]), 0.0)
    sums[...] = jnp.broadcast_to(row, sums.shape)


VMEM = pl.BlockSpec(memory_space=pltpu.VMEM)
SMEM = pl.BlockSpec(memory_space=pltpu.SMEM)
PARAMS = pltpu.CompilerParams(vmem_limit_bytes=48 * 1024 * 1024)


def f32(*shape):
    return jax.ShapeDtypeStruct(shape, jnp.float32)


def rows(u):
    lead = u.shape[:-2]
    n = len(lead)
    return u.reshape(*lead, 2, 8, 128).transpose(*range(n), n + 1, n, n + 2).reshape(*lead, 16, 128)


def unrows(u):
    lead = u.shape[:-2]
    n = len(lead)
    return u.reshape(*lead, 8, 2, 128).transpose(*range(n), n + 1, n, n + 2).reshape(*lead, 2, 1024)


def swap_pairs(value, axes, odd):
    size = lax.axis_size(axes)
    pairs = []
    for low in range(odd, size - 1, 2):
        pairs += [(low, low + 1), (low + 1, low)]
    return lax.ppermute(value, axes, pairs)


def spread_sum(value, axes):
    size = lax.axis_size(axes)
    sent = jnp.broadcast_to(value[None], (size, value.shape[0]))
    return jnp.sum(lax.all_to_all(sent, axes, 0, 0), axis=0)


def body(e_check, h_check, adj_e, adj_h, material, owner, permittivity):
    e, h, g, k, m, own = (rows(u) for u in (e_check, h_check, adj_e, adj_h, material, owner))
    first = pl.BlockSpec((3, 2, 16, 128), lambda i: (0, 0, 0, 0))
    last = pl.BlockSpec((3, 2, 16, 128), lambda i: (0, 3, 0, 0))
    pair, following = pl.pallas_call(
        pack_kernel,
        grid=(1,),
        out_shape=(f32(HALO, 16, 128), f32(HALO, 16, 128)),
        in_specs=[SMEM] + [first, last] * 4
        + [pl.BlockSpec((2, 16, 128), lambda i: (0, 0, 0)), pl.BlockSpec((2, 16, 128), lambda i: (3, 0, 0))],
        out_specs=[pl.BlockSpec((HALO, 16, 128), lambda i: (0, 0, 0))] * 2,
        compiler_params=PARAMS,
        name="pack",
    )(permittivity, e, e, h, h, g, g, k, k, m, m)
    following = swap_pairs(following, XY, 1)
    pair = swap_pairs(pair, "c", 0)
    pay0, pay1, t1s, s1s, s0s, cs = pl.pallas_call(
        local_kernel,
        out_shape=(
            f32(LINES, 8, 128),
            f32(LINES, 8, 128),
            f32(2, 3, 2, 11, 8, 128),
            f32(2, 3, 2, 10, 8, 128),
            f32(2, 2, 10, 8, 128),
            f32(2, 10, 8, 128),
        ),
        in_specs=[SMEM] + [VMEM] * 7,
        out_specs=[VMEM] * 6,
        compiler_params=PARAMS,
        name="local_step",
    )(permittivity, e, h, g, k, m, pair, following)
    pay1 = swap_pairs(pay1, GZ, 1)
    pay0 = swap_pairs(pay0, "x", 0)
    out_e, out_h, sums = pl.pallas_call(
        final_kernel,
        out_shape=(f32(3, 8, 16, 128), f32(3, 8, 16, 128), f32(1, 128)),
        in_specs=[SMEM] + [VMEM] * 10,
        out_specs=[VMEM] * 3,
        compiler_params=PARAMS,
        name="final_step",
    )(permittivity, e, g, m, own, pay0, pay1, t1s, s1s, s0s, cs)
    total = spread_sum(sums[0], ("zl", "zh", "c"))
    total = spread_sum(total, ("y", "x"))
    cells = 8 * lax.axis_size(XY) * 2 * lax.axis_size(GZ) * 1024
    gradient = total[:NI] / jnp.sqrt(jnp.float32(cells / NI))
    return unrows(out_e), unrows(out_h), gradient


def on_split(split):
    return jax.shard_map(
        body,
        mesh=split,
        in_specs=(P(None, XY, GZ, None),) * 4 + (P(XY, GZ, None),) * 2 + (P(),),
        out_specs=(P(None, XY, GZ, None), P(None, XY, GZ, None), P()),
        check_vma=False,
    )


def solution(mesh):
    return on_split(Mesh(mesh.devices.reshape(4, 8, 2, 2, 4), AXES))
```

time: 123 us -> 83.2 us (0.68); the launches traced: 121 us -> 82.7 us
  starting transfers between devices: 29.9 us -> 13.4 us
  blocking collectives: 60.4 us -> 48.3 us
  other arithmetic: 9.33 us -> 0.55 us
  Pallas kernels: 0 us -> 3.48 us
  between operations: 4 us -> 0.73 us
  matrix products: 1.4 us -> 0 us
    psum x5 -> x0, blocking collectives: 60.4 us -> none  [one_axis_at_a_time(): return functools.reduce(lax.psum, axes, x)]
    all_to_all x0 -> x2, blocking collectives: none -> 48.3 us  [spread_sum(): return jnp.sum(lax.all_to_all(sent, axes, 0, 0), axis=0)]
    ppermute x8 -> x4, starting transfers between devices: 29.9 us -> 13.4 us  [swap_pairs(): return lax.ppermute(value, axes, pairs)]
    another operation x24 -> x0, other arithmetic: 5.72 us -> none  [the longest x8 1.96 us: body(): first = curl_fwd(jnp.stack([electric[-1], e_coef * adjoint_e[-1]], axis=0))]
    pallas_call x0 -> x3, Pallas kernels: none -> 3.48 us  [the longest x1 1.89 us: body(): pl.pallas_call(final_kernel, out_shape=(f32(3, 8, 16, 128), f32(3, 8, 16,...]
    unnamed x15 -> x18, local copies, waits for them, and re-layouts: 2.36 us -> 5.21 us
    slice x17 -> x0, local copies, waits for them, and re-layouts: 2.57 us -> none  [the longest x1 1.47 us: body(): permittivity[kind_index]]
    dot_general x2 -> x0, matrix products: 1.4 us -> none  [interface_sums(): jnp.dot(weight.reshape(1, -1), onehot, precision=lax.Precision.HIGHEST)[0]]
  transfers between devices with their start and end apart: 8 -> 4, of which waited for: 3 -> 2; matrix products, arithmetic and copies ran while one was open for 2% -> 0% of each run, Pallas kernels for 0% -> 0%
where the time goes in v1:
time: 83.2 us; the launch traced here: 82.7 us
  blocking collectives  48.3 us (58%)
  starting transfers between devices  13.4 us (16%)
  waiting for transfers between devices  10.9 us (13%)
  local copies, waits for them, and re-layouts  5.23 us (6%)
  Pallas kernels  3.48 us (4%)
    all_to_all x2, blocking collectives, spread_sum(): return jnp.sum(lax.all_to_all(sent, axes, 0, 0), axis=0)  48.3 us
    ppermute x4, starting transfers between devices, swap_pairs(): return lax.ppermute(value, axes, pairs)  13.4 us
    ppermute x4, waiting for transfers between devices, swap_pairs(): return lax.ppermute(value, axes, pairs)  10.9 us
    unnamed x18, local copies, waits for them, and re-layouts  5.21 us
    pallas_call x1, Pallas kernels, body(): pl.pallas_call(final_kernel, out_shape=(f32(3, 8, 16, 128), f32(3, 8, 16,...  1.89 us
  transfers between devices with their start and end apart: 4, of which 2 were waited for; matrix products, arithmetic and copies ran while one was open for 0% of the time, Pallas kernels for 0%

profile of v1, /device:TPU:1, one launch (start us, length us, event | category | flops | bytes accessed | tf_op | source)
XLA Modules:
  0.0 82.7 jit_solution(10230532770093350964)
XLA Ops:
  0.6 0.0 copy-start.8
  0.6 0.6 copy-done.8
  1.3 0.0 copy-start
  1.3 0.9 %copy-done = f32[3,8,2,1024]{3,2,1,0:T(2,128)S(1)} copy-done((f32[3,8,2,1024]{3,2,1,0:T(2,128)S(1)}, f32[3,8,2,1024]{3,2,1,0:T(2,128)}, u32[]{:S(2)}) %copy-start) | copy-done | bytes 196632
  2.2 0.0 copy-start.1
  2.2 0.9 %copy-done.1 = f32[3,8,2,1024]{3,2,1,0:T(2,128)S(1)} copy-done((f32[3,8,2,1024]{3,2,1,0:T(2,128)S(1)}, f32[3,8,2,1024]{3,2,1,0:T(2,128)}, u32[]{:S(2)}) %copy-start.1) | copy-done | bytes 196632
  3.1 0.0 copy-start.3
  3.1 0.9 %copy-done.3 = f32[3,8,2,1024]{3,2,1,0:T(2,128)S(1)} copy-done((f32[3,8,2,1024]{3,2,1,0:T(2,128)S(1)}, f32[3,8,2,1024]{3,2,1,0:T(2,128)}, u32[]{:S(2)}) %copy-start.3) | copy-done | bytes 196632
  4.1 0.0 copy-start.4
  4.1 0.9 %copy-done.4 = f32[3,8,2,1024]{3,2,1,0:T(2,128)S(1)} copy-done((f32[3,8,2,1024]{3,2,1,0:T(2,128)S(1)}, f32[3,8,2,1024]{3,2,1,0:T(2,128)}, u32[]{:S(2)}) %copy-start.4) | copy-done | bytes 196632
  5.0 0.0 copy-start.5
  5.0 0.8 %copy-done.5 = s32[8,2,1024]{2,1,0:T(2,128)S(1)} copy-done((s32[8,2,1024]{2,1,0:T(2,128)S(1)}, s32[8,2,1024]{2,1,0:T(2,128)}, u32[]{:S(2)}) %copy-start.5) | copy-done | bytes 65560
  5.8 0.6 pack.1
  6.4 8.8 %collective-permute-start = (f32[26,16,128]{2,1,0:T(8,128)S(1)}, f32[26,16,128]{2,1,0:T(8,128)S(1)}, u32[]{:S(2)}, u32[]{:S(2)}) collective-permute-start(f32[26,16,128]{2,1,0:T(8,128)S(1)} %get-tuple-element.14), channel_id=1, source_target_pairs={{0,8},{8,0},{1,9},{9,1},{2,10},{10,2},{3,11},{11,3},{4,12},{12,4},... | collective-permute-start | bytes 638984 | tf_op jit(solution)/shard_map/ppermute | solution.py:267
  15.2 0.0 copy-start.2
  15.2 0.0 copy-start.6
  15.3 0.0 copy-start.7
  15.3 2.1 %collective-permute-start.1 = (f32[26,16,128]{2,1,0:T(8,128)S(1)}, f32[26,16,128]{2,1,0:T(8,128)S(1)}, u32[]{:S(2)}, u32[]{:S(2)}) collective-permute-start(f32[26,16,128]{2,1,0:T(8,128)S(1)} %get-tuple-element.15), channel_id=1, source_target_pairs={{8,16},{16,8},{24,32},{32,24},{40,48},{48,40},{56,64},{64,56},{72,... | collective-permute-start | bytes 638984 | tf_op jit(solution)/shard_map/ppermute | solution.py:267
  17.3 0.0 collective-permute-done.pair_ref
  17.3 5.5 %collective-permute-done.1.next_ref = f32[26,16,128]{2,1,0:T(8,128)S(1)} collective-permute-done((f32[26,16,128]{2,1,0:T(8,128)S(1)}, f32[26,16,128]{2,1,0:T(8,128)S(1)}, u32[]{:S(2)}, u32[]{:S(2)}) %collective-permute-start.1) | collective-permute-done | bytes 213024 | tf_op jit(solution)/shard_map/ppermute | solution.py:267
  22.9 1.0 %local_step.1 = (f32[85,8,128]{2,1,0:T(8,128)S(1)}, f32[85,8,128]{2,1,0:T(8,128)S(1)}, f32[2,3,2,11,8,128]{5,4,3,2,1,0:T(8,128)S(1)}, f32[2,3,2,10,8,128]{5,4,3,...) custom-call(f32[4]{0:T(128)S(1)} %copy-done.8, f32[3,8,16,128]{3,2,1,0:T(8,128)S(1)} %bitcast.45, ...), custom_call_target="tpu_custom_call" | custom-call | tf_op jit(solution)/shard_map/local_step/pallas_call | solution.py:292
  23.9 1.9 %collective-permute-start.2 = (f32[85,8,128]{2,1,0:T(8,128)S(1)}, f32[85,8,128]{2,1,0:T(8,128)S(1)}, u32[]{:S(2)}, u32[]{:S(2)}) collective-permute-start(f32[85,8,128]{2,1,0:T(8,128)S(1)} %get-tuple-element.16), channel_id=1, source_target_pairs={{0,1},{1,0},{2,3},{3,2},{4,5},{5,4},{6,7},{7,6},{8,9},{9,8},{10,11... | collective-permute-start | bytes 1044488 | tf_op jit(solution)/shard_map/ppermute | solution.py:267
  25.8 0.7 collective-permute-start.3
  26.5 5.4 %collective-permute-done.2.r0 = f32[85,8,128]{2,1,0:T(8,128)S(1)} collective-permute-done((f32[85,8,128]{2,1,0:T(8,128)S(1)}, f32[85,8,128]{2,1,0:T(8,128)S(1)}, u32[]{:S(2)}, u32[]{:S(2)}) %collective-permute-start.2) | collective-permute-done | bytes 348192 | tf_op jit(solution)/shard_map/ppermute | solution.py:267
  31.9 0.0 collective-permute-done.3.r1
  31.9 0.0 copy-done.2
  31.9 0.0 copy-done.6
  31.9 0.0 copy-done.7
  31.9 1.9 %final_step.1 = (f32[3,8,16,128]{3,2,1,0:T(8,128)}, f32[3,8,16,128]{3,2,1,0:T(8,128)}, f32[1,128]{1,0:T(1,128)S(1)}) custom-call(f32[4]{0:T(128)S(1)} %copy-done.8, f32[3,8,16,128]{3,2,1,0:T(8,128)S(1)} %bitcast.46, f32[3,8,16,128]{3,2,1,0:T(8,128)S(1)} %bitcast.50, s32[8,16,128]{2,1,0:T(8,128)S(1)} %bitcast.60, s32[8,16,128]{2,1,0:T(8,128)S(1)} %bitcast.61, ...), custom_call_target="tpu_custom_call" | custom-call | tf_op jit(solution)/shard_map/final_step/pallas_call | solution.py:309
  33.8 32.8 %all_to_all.12 = f32[16,1,128]{2,1,0:T(1,128)S(1)} all-to-all(f32[16,1,128]{2,1,0:T(1,128)S(1)} %broadcast_in_dim.4), channel_id=1, replica_groups=mesh['zl'=4,'y'=8,'c'=2,'zh'=2,'x'=4] {'zl','zh','c'}, dimensions={0} | all-to-all | bytes 16384 | tf_op jit(solution)/shard_map/all_to_all | solution.py:273
  66.6 15.6 %all_to_all.13 = f32[32,1,128]{2,1,0:T(1,128)S(1)} all-to-all(f32[32,1,128]{2,1,0:T(1,128)S(1)} %broadcast_in_dim.5), channel_id=1, replica_groups=mesh['zl'=4,'y'=8,'c'=2,'zh'=2,'x'=4] {'y','x'}, dimensions={0} | all-to-all | bytes 32768 | tf_op jit(solution)/shard_map/all_to_all | solution.py:273
  82.2 0.5 slice_multiply_fusion
  (4 shorter events, 0.1 us)
Async XLA Ops:
  0.6 0.7 copy-start.8
  1.3 0.9 %copy-start = (f32[3,8,2,1024]{3,2,1,0:T(2,128)S(1)}, f32[3,8,2,1024]{3,2,1,0:T(2,128)}, u32[]{:S(2)}) copy-start(f32[3,8,2,1024]{3,2,1,0:T(2,128)} %param.7) | copy-start | bytes 589828
  2.2 0.9 %copy-start.1 = (f32[3,8,2,1024]{3,2,1,0:T(2,128)S(1)}, f32[3,8,2,1024]{3,2,1,0:T(2,128)}, u32[]{:S(2)}) copy-start(f32[3,8,2,1024]{3,2,1,0:T(2,128)} %param.9) | copy-start | bytes 589828
  3.1 0.9 %copy-start.3 = (f32[3,8,2,1024]{3,2,1,0:T(2,128)S(1)}, f32[3,8,2,1024]{3,2,1,0:T(2,128)}, u32[]{:S(2)}) copy-start(f32[3,8,2,1024]{3,2,1,0:T(2,128)} %param.8) | copy-start | bytes 589828
  4.1 0.9 %copy-start.4 = (f32[3,8,2,1024]{3,2,1,0:T(2,128)S(1)}, f32[3,8,2,1024]{3,2,1,0:T(2,128)}, u32[]{:S(2)}) copy-start(f32[3,8,2,1024]{3,2,1,0:T(2,128)} %param.10) | copy-start | bytes 589828
  5.0 0.8 %copy-start.5 = (s32[8,2,1024]{2,1,0:T(2,128)S(1)}, s32[8,2,1024]{2,1,0:T(2,128)}, u32[]{:S(2)}) copy-start(s32[8,2,1024]{2,1,0:T(2,128)} %param.11) | copy-start | bytes 196612
  6.4 10.9 %collective-permute-start = (f32[26,16,128]{2,1,0:T(8,128)S(1)}, f32[26,16,128]{2,1,0:T(8,128)S(1)}, u32[]{:S(2)}, u32[]{:S(2)}) collective-permute-start(f32[26,16,128]{2,1,0:T(8,128)S(1)} %get-tuple-element.14), channel_id=1, source_target_pairs={{0,8},{8,0},{1,9},{9,1},{2,10},{10,2},{3,11},{11,3},{4,12},{12,4},... | collective-permute-start | bytes 638984 | tf_op jit(solution)/shard_map/ppermute | solution.py:267
  15.2 16.7 %copy-start.2 = (f32[3,8,2,1024]{3,2,1,0:T(2,128)S(1)}, f32[3,8,2,1024]{3,2,1,0:T(2,128)}, u32[]{:S(2)}) copy-start(f32[3,8,2,1024]{3,2,1,0:T(2,128)} %param.9) | copy-start | bytes 589828
  15.2 16.7 %copy-start.6 = (s32[8,2,1024]{2,1,0:T(2,128)S(1)}, s32[8,2,1024]{2,1,0:T(2,128)}, u32[]{:S(2)}) copy-start(s32[8,2,1024]{2,1,0:T(2,128)} %param.11) | copy-start | bytes 196612
  15.3 16.6 %copy-start.7 = (s32[8,2,1024]{2,1,0:T(2,128)S(1)}, s32[8,2,1024]{2,1,0:T(2,128)}, u32[]{:S(2)}) copy-start(s32[8,2,1024]{2,1,0:T(2,128)} %param.12) | copy-start | bytes 196612
  15.3 7.6 %collective-permute-start.1 = (f32[26,16,128]{2,1,0:T(8,128)S(1)}, f32[26,16,128]{2,1,0:T(8,128)S(1)}, u32[]{:S(2)}, u32[]{:S(2)}) collective-permute-start(f32[26,16,128]{2,1,0:T(8,128)S(1)} %get-tuple-element.15), channel_id=1, source_target_pairs={{8,16},{16,8},{24,32},{32,24},{40,48},{48,40},{56,64},{64,56},{72,... | collective-permute-start | bytes 638984 | tf_op jit(solution)/shard_map/ppermute | solution.py:267
  23.9 8.0 %collective-permute-start.2 = (f32[85,8,128]{2,1,0:T(8,128)S(1)}, f32[85,8,128]{2,1,0:T(8,128)S(1)}, u32[]{:S(2)}, u32[]{:S(2)}) collective-permute-start(f32[85,8,128]{2,1,0:T(8,128)S(1)} %get-tuple-element.16), channel_id=1, source_target_pairs={{0,1},{1,0},{2,3},{3,2},{4,5},{5,4},{6,7},{7,6},{8,9},{9,8},{10,11... | collective-permute-start | bytes 1044488 | tf_op jit(solution)/shard_map/ppermute | solution.py:267
  25.8 6.1 %collective-permute-start.3 = (f32[85,8,128]{2,1,0:T(8,128)S(1)}, f32[85,8,128]{2,1,0:T(8,128)S(1)}, u32[]{:S(2)}, u32[]{:S(2)}) collective-permute-start(f32[85,8,128]{2,1,0:T(8,128)S(1)} %get-tuple-element.17), channel_id=1, source_target_pairs={{1,2},{2,1},{3,4},{4,3},{5,6},{6,5},{9,10},{10,9},{11,12},{12,11},... | collective-permute-start | bytes 1044488 | tf_op jit(solution)/shard_map/ppermute | solution.py:267

commit v2 on v1

--- a/solution.py
+++ b/solution.py
@@ -70,23 +70,34 @@
     return jnp.where(first, 0.0, 1.0).astype(jnp.float32)
 
 
-def pack_kernel(eps_ref, e0, e1, h0, h1, g0, g1, k0, k1, m0, m1, pair_ref, next_ref):
+def pack_kernel(eps_ref, e, h, g, k, m, pair_ref, next_ref, eps, strips, kinds, sems):
+    copies = [pltpu.make_async_copy(eps_ref, eps, sems.at[10])]
+    for side, start in enumerate((0, 6)):
+        for field, ref in enumerate((e, h, g, k)):
+            copies.append(
+                pltpu.make_async_copy(ref.at[:, start : start + 2], strips.at[side, field], sems.at[side * 5 + field])
+            )
+        copies.append(pltpu.make_async_copy(m.at[start : start + 2], kinds.at[side], sems.at[side * 5 + 4]))
+    for copy in copies:
+        copy.start()
+    for copy in copies:
+        copy.wait()
     even = lax.axis_index("c") == 0
-    values = coefs(eps_ref)
+    values = coefs(eps)
 
     def put(row, first, last):
         pair_ref[row] = jnp.where(even, last, first)
         next_ref[row] = jnp.where(even, first, last)
 
-    for field, (first, last) in enumerate(((e0, e1), (h0, h1), (g0, g1), (k0, k1))):
+    for field in range(4):
         for comp in range(3):
-            for k in range(2):
-                put(field * 6 + comp * 2 + k, first[comp, k], last[comp, k])
-    for k in range(2):
-        put(24 + k, table(m0[k], values), table(m1[k], values))
-
-
-def local_kernel(eps_ref, e, h, g, kf, m, pair_ref, next_ref, pay0, pay1, t1s, s1s, s0s, cs):
+            for line in range(2):
+                put(field * 6 + comp * 2 + line, strips[0, field, comp, line], strips[1, field, comp, line])
+    for line in range(2):
+        put(24 + line, table(kinds[0, line], values), table(kinds[1, line], values))
+
+
+def local_kernel(eps_ref, e, h, g, kf, m, next_ref, pair_ref, pay0, pay1, t1s, s1s, s0s, cs):
     even_x = lax.axis_index("c") == 0
     even_z = lax.axis_index("x") % 2 == 0
     x_flag = low_flag(XY)
@@ -156,7 +167,7 @@
     put(pl.ds(76, 9), coef[1][2:11], coef[0][1:10])
 
 
-def final_kernel(eps_ref, e, g, m, owner, r0, r1, t1s, s1s, s0s, cs, adj_e, adj_h, sums):
+def final_kernel(eps_ref, e, g, m, owner, r1, r0, t1s, s1s, s0s, cs, adj_e, adj_h, sums):
     even_z = lax.axis_index("x") % 2 == 0
     x_flag, z_flag = low_flag(XY), low_flag(GZ)
     values = coefs(eps_ref)
@@ -240,6 +251,8 @@
 
 VMEM = pl.BlockSpec(memory_space=pltpu.VMEM)
 SMEM = pl.BlockSpec(memory_space=pltpu.SMEM)
+HBM = pl.BlockSpec(memory_space=pltpu.HBM)
+LARGE = 62 * 1024 * 1024
 PARAMS = pltpu.CompilerParams(vmem_limit_bytes=48 * 1024 * 1024)
 
 
@@ -275,20 +288,22 @@
 
 def body(e_check, h_check, adj_e, adj_h, material, owner, permittivity):
     e, h, g, k, m, own = (rows(u) for u in (e_check, h_check, adj_e, adj_h, material, owner))
-    first = pl.BlockSpec((3, 2, 16, 128), lambda i: (0, 0, 0, 0))
-    last = pl.BlockSpec((3, 2, 16, 128), lambda i: (0, 3, 0, 0))
     pair, following = pl.pallas_call(
         pack_kernel,
-        grid=(1,),
         out_shape=(f32(HALO, 16, 128), f32(HALO, 16, 128)),
-        in_specs=[SMEM] + [first, last] * 4
-        + [pl.BlockSpec((2, 16, 128), lambda i: (0, 0, 0)), pl.BlockSpec((2, 16, 128), lambda i: (3, 0, 0))],
-        out_specs=[pl.BlockSpec((HALO, 16, 128), lambda i: (0, 0, 0))] * 2,
-        compiler_params=PARAMS,
+        in_specs=[HBM] * 6,
+        out_specs=[VMEM] * 2,
+        scratch_shapes=[
+            pltpu.SMEM((4,), jnp.float32),
+            pltpu.VMEM((2, 4, 3, 2, 16, 128), jnp.float32),
+            pltpu.VMEM((2, 2, 16, 128), jnp.int32),
+            pltpu.SemaphoreType.DMA((11,)),
+        ],
+        compiler_params=pltpu.CompilerParams(vmem_limit_bytes=LARGE),
         name="pack",
-    )(permittivity, e, e, h, h, g, g, k, k, m, m)
+    )(permittivity, e, h, g, k, m)
+    pair = swap_pairs(pair, "c", 0)
     following = swap_pairs(following, XY, 1)
-    pair = swap_pairs(pair, "c", 0)
     pay0, pay1, t1s, s1s, s0s, cs = pl.pallas_call(
         local_kernel,
         out_shape=(
@@ -303,9 +318,9 @@
         out_specs=[VMEM] * 6,
         compiler_params=PARAMS,
         name="local_step",
-    )(permittivity, e, h, g, k, m, pair, following)
+    )(permittivity, e, h, g, k, m, following, pair)
+    pay0 = swap_pairs(pay0, "x", 0)
     pay1 = swap_pairs(pay1, GZ, 1)
-    pay0 = swap_pairs(pay0, "x", 0)
     out_e, out_h, sums = pl.pallas_call(
         final_kernel,
         out_shape=(f32(3, 8, 16, 128), f32(3, 8, 16, 128), f32(1, 128)),
@@ -313,7 +328,7 @@
         out_specs=[VMEM] * 3,
         compiler_params=PARAMS,
         name="final_step",
-    )(permittivity, e, g, m, own, pay0, pay1, t1s, s1s, s0s, cs)
+    )(permittivity, e, g, m, own, pay1, pay0, t1s, s1s, s0s, cs)
     total = spread_sum(sums[0], ("zl", "zh", "c"))
     total = spread_sum(total, ("y", "x"))
     cells = 8 * lax.axis_size(XY) * 2 * lax.axis_size(GZ) * 1024

time: 83.2 us -> 73.6 us (0.88)
  local copies, waits for them, and re-layouts: 5.23 us -> 0.05 us
  blocking collectives: 48.3 us -> 44.3 us
  waiting for transfers between devices: 10.9 us -> 9.47 us
  Pallas kernels: 3.48 us -> 4.8 us
    unnamed x18 -> x14, local copies, waits for them, and re-layouts: 5.21 us -> 0.03 us
    all_to_all x2, blocking collectives: 48.3 us -> 44.3 us  [spread_sum(): return jnp.sum(lax.all_to_all(sent, axes, 0, 0), axis=0)]
    ppermute x4, waiting for transfers between devices: 10.9 us -> 9.47 us  [swap_pairs(): return lax.ppermute(value, axes, pairs)]
    pallas_call x1, Pallas kernels: 0.6 us -> 1.96 us  [body(): pl.pallas_call(pack_kernel, out_shape=(f32(HALO, 16, 128), f32(HALO, 16,...]
where the time goes in v2:
time: 73.6 us; the launch traced here: 73.3 us
  blocking collectives  44.3 us (60%)
  starting transfers between devices  13.3 us (18%)
  waiting for transfers between devices  9.47 us (13%)
  Pallas kernels  4.8 us (7%)
  between operations  0.77 us (1%)
    all_to_all x2, blocking collectives, spread_sum(): return jnp.sum(lax.all_to_all(sent, axes, 0, 0), axis=0)  44.3 us
    ppermute x4, starting transfers between devices, swap_pairs(): return lax.ppermute(value, axes, pairs)  13.3 us
    ppermute x4, waiting for transfers between devices, swap_pairs(): return lax.ppermute(value, axes, pairs)  9.47 us
    pallas_call x1, Pallas kernels, body(): pl.pallas_call(pack_kernel, out_shape=(f32(HALO, 16, 128), f32(HALO, 16,...  1.96 us
    pallas_call x1, Pallas kernels, body(): pl.pallas_call(final_kernel, out_shape=(f32(3, 8, 16, 128), f32(3, 8, 16,...  1.85 us
  transfers between devices with their start and end apart: 4, of which 2 were waited for; matrix products, arithmetic and copies ran while one was open for 0% of the time, Pallas kernels for 0%

profile of v2, /device:TPU:1, one launch (start us, length us, event | category | flops | bytes accessed | tf_op | source)
XLA Modules:
  0.0 73.3 jit_solution(7758520339140089833)
XLA Ops:
  0.6 0.0 copy-start
  0.6 0.0 copy-start.1
  0.7 0.0 copy-start.2
  0.7 0.0 copy-start.3
  0.7 0.0 copy-start.4
  0.7 2.0 %pack.1 = (f32[26,16,128]{2,1,0:T(8,128)}, f32[26,16,128]{2,1,0:T(8,128)}) custom-call(f32[4]{0:T(128)} %eps_ref.5, f32[3,8,16,128]{3,2,1,0:T(8,128)} %bitcast.43, f32[3,8,16,128]{3,2,1,0:T(8,128)} %bitcast.49, f32[3,8,16,128]{3,2,1,0:T(8,128)} %bitcast.46, f32[3,8,16,128]{3,2,1,0:T(8,128)} %bitcast.51, s32[8,16,128]{2,1,0:T(8,128)} %bitcast.53), custom_call_target="tpu_custom_call" | custom-call | tf_op jit(solution)/shard_map/pack/pallas_call | solution.py:291
  2.7 0.0 copy-start.6
  2.7 4.6 %collective-permute-start = (f32[26,16,128]{2,1,0:T(8,128)}, f32[26,16,128]{2,1,0:T(8,128)S(1)}, u32[]{:S(2)}, u32[]{:S(2)}) collective-permute-start(f32[26,16,128]{2,1,0:T(8,128)} %get-tuple-element.14), channel_id=1, source_target_pairs={{8,16},{16,8},{24,32},{32,24},{40,48},{48,40},{56,64},{64,56},{72,... | collective-permute-start | bytes 638984 | tf_op jit(solution)/shard_map/ppermute | solution.py:280
  7.3 0.0 copy-start.5
  7.3 5.0 %collective-permute-start.1 = (f32[26,16,128]{2,1,0:T(8,128)}, f32[26,16,128]{2,1,0:T(8,128)S(1)}, u32[]{:S(2)}, u32[]{:S(2)}) collective-permute-start(f32[26,16,128]{2,1,0:T(8,128)} %get-tuple-element.15), channel_id=1, source_target_pairs={{0,8},{8,0},{1,9},{9,1},{2,10},{10,2},{3,11},{11,3},{4,12},{12,4},... | collective-permute-start | bytes 638984 | tf_op jit(solution)/shard_map/ppermute | solution.py:280
  12.3 0.0 collective-permute-done.next_ref
  12.3 1.3 %collective-permute-done.1.pair_ref = f32[26,16,128]{2,1,0:T(8,128)S(1)} collective-permute-done((f32[26,16,128]{2,1,0:T(8,128)}, f32[26,16,128]{2,1,0:T(8,128)S(1)}, u32[]{:S(2)}, u32[]{:S(2)}) %collective-permute-start.1) | collective-permute-done | bytes 213024 | tf_op jit(solution)/shard_map/ppermute | solution.py:280
  13.6 0.0 copy-done
  13.6 0.0 copy-done.1
  13.6 0.0 copy-done.2
  13.6 0.0 copy-done.3
  13.6 0.0 copy-done.4
  13.6 0.0 copy-done.6
  13.6 1.0 %local_step.1 = (f32[85,8,128]{2,1,0:T(8,128)S(1)}, f32[85,8,128]{2,1,0:T(8,128)S(1)}, f32[2,3,2,11,8,128]{5,4,3,2,1,0:T(8,128)S(1)}, f32[2,3,2,10,8,128]{5,4,3,...) custom-call(f32[4]{0:T(128)S(1)} %copy-done.6, f32[3,8,16,128]{3,2,1,0:T(8,128)S(1)} %bitcast.44, ...), custom_call_target="tpu_custom_call" | custom-call | tf_op jit(solution)/shard_map/local_step/pallas_call | solution.py:307
  14.6 0.7 collective-permute-start.2
  15.3 3.0 %collective-permute-start.3 = (f32[85,8,128]{2,1,0:T(8,128)S(1)}, f32[85,8,128]{2,1,0:T(8,128)S(1)}, u32[]{:S(2)}, u32[]{:S(2)}) collective-permute-start(f32[85,8,128]{2,1,0:T(8,128)S(1)} %get-tuple-element.17), channel_id=1, source_target_pairs={{0,1},{1,0},{2,3},{3,2},{4,5},{5,4},{6,7},{7,6},{8,9},{9,8},{10,11... | collective-permute-start | bytes 1044488 | tf_op jit(solution)/shard_map/ppermute | solution.py:280
  18.3 0.0 collective-permute-done.2.r1
  18.3 8.2 %collective-permute-done.3.r0 = f32[85,8,128]{2,1,0:T(8,128)S(1)} collective-permute-done((f32[85,8,128]{2,1,0:T(8,128)S(1)}, f32[85,8,128]{2,1,0:T(8,128)S(1)}, u32[]{:S(2)}, u32[]{:S(2)}) %collective-permute-start.3) | collective-permute-done | bytes 348192 | tf_op jit(solution)/shard_map/ppermute | solution.py:280
  26.5 0.0 copy-done.5
  26.5 1.9 %final_step.1 = (f32[3,8,16,128]{3,2,1,0:T(8,128)}, f32[3,8,16,128]{3,2,1,0:T(8,128)}, f32[1,128]{1,0:T(1,128)S(1)}) custom-call(f32[4]{0:T(128)S(1)} %copy-done.6, f32[3,8,16,128]{3,2,1,0:T(8,128)S(1)} %bitcast.45, f32[3,8,16,128]{3,2,1,0:T(8,128)S(1)} %bitcast.48, s32[8,16,128]{2,1,0:T(8,128)S(1)} %bitcast.55, s32[8,16,128]{2,1,0:T(8,128)S(1)} %bitcast.56, ...), custom_call_target="tpu_custom_call" | custom-call | tf_op jit(solution)/shard_map/final_step/pallas_call | solution.py:324
  28.4 29.9 %all_to_all.12 = f32[16,1,128]{2,1,0:T(1,128)S(1)} all-to-all(f32[16,1,128]{2,1,0:T(1,128)S(1)} %broadcast_in_dim.4), channel_id=1, replica_groups=mesh['zl'=4,'y'=8,'c'=2,'zh'=2,'x'=4] {'zl','zh','c'}, dimensions={0} | all-to-all | bytes 16384 | tf_op jit(solution)/shard_map/all_to_all | solution.py:286
  58.3 14.5 %all_to_all.13 = f32[32,1,128]{2,1,0:T(1,128)S(1)} all-to-all(f32[32,1,128]{2,1,0:T(1,128)S(1)} %broadcast_in_dim.5), channel_id=1, replica_groups=mesh['zl'=4,'y'=8,'c'=2,'zh'=2,'x'=4] {'y','x'}, dimensions={0} | all-to-all | bytes 32768 | tf_op jit(solution)/shard_map/all_to_all | solution.py:286
  72.8 0.5 slice_multiply_fusion
  (4 shorter events, 0.1 us)
Async XLA Ops:
  0.6 12.9 %copy-start = (f32[3,8,2,1024]{3,2,1,0:T(2,128)S(1)}, f32[3,8,2,1024]{3,2,1,0:T(2,128)}, u32[]{:S(2)}) copy-start(f32[3,8,2,1024]{3,2,1,0:T(2,128)} %param.7) | copy-start | bytes 589828
  0.6 12.9 %copy-start.1 = (f32[3,8,2,1024]{3,2,1,0:T(2,128)S(1)}, f32[3,8,2,1024]{3,2,1,0:T(2,128)}, u32[]{:S(2)}) copy-start(f32[3,8,2,1024]{3,2,1,0:T(2,128)} %param.9) | copy-start | bytes 589828
  0.7 12.9 %copy-start.2 = (f32[3,8,2,1024]{3,2,1,0:T(2,128)S(1)}, f32[3,8,2,1024]{3,2,1,0:T(2,128)}, u32[]{:S(2)}) copy-start(f32[3,8,2,1024]{3,2,1,0:T(2,128)} %param.8) | copy-start | bytes 589828
  0.7 12.9 %copy-start.3 = (f32[3,8,2,1024]{3,2,1,0:T(2,128)S(1)}, f32[3,8,2,1024]{3,2,1,0:T(2,128)}, u32[]{:S(2)}) copy-start(f32[3,8,2,1024]{3,2,1,0:T(2,128)} %param.10) | copy-start | bytes 589828
  0.7 12.9 %copy-start.4 = (s32[8,2,1024]{2,1,0:T(2,128)S(1)}, s32[8,2,1024]{2,1,0:T(2,128)}, u32[]{:S(2)}) copy-start(s32[8,2,1024]{2,1,0:T(2,128)} %param.11) | copy-start | bytes 196612
  2.7 10.9 %copy-start.6 = (f32[4]{0:T(128)S(1)}, f32[4]{0:T(128)}, u32[]{:S(2)}) copy-start(f32[4]{0:T(128)} %eps_ref.5) | copy-start | bytes 52
  2.7 9.6 %collective-permute-start = (f32[26,16,128]{2,1,0:T(8,128)}, f32[26,16,128]{2,1,0:T(8,128)S(1)}, u32[]{:S(2)}, u32[]{:S(2)}) collective-permute-start(f32[26,16,128]{2,1,0:T(8,128)} %get-tuple-element.14), channel_id=1, source_target_pairs={{8,16},{16,8},{24,32},{32,24},{40,48},{48,40},{56,64},{64,56},{72,... | collective-permute-start | bytes 638984 | tf_op jit(solution)/shard_map/ppermute | solution.py:280
  7.3 19.2 %copy-start.5 = (s32[8,2,1024]{2,1,0:T(2,128)S(1)}, s32[8,2,1024]{2,1,0:T(2,128)}, u32[]{:S(2)}) copy-start(s32[8,2,1024]{2,1,0:T(2,128)} %param.12) | copy-start | bytes 196612
  7.3 6.3 %collective-permute-start.1 = (f32[26,16,128]{2,1,0:T(8,128)}, f32[26,16,128]{2,1,0:T(8,128)S(1)}, u32[]{:S(2)}, u32[]{:S(2)}) collective-permute-start(f32[26,16,128]{2,1,0:T(8,128)} %get-tuple-element.15), channel_id=1, source_target_pairs={{0,8},{8,0},{1,9},{9,1},{2,10},{10,2},{3,11},{11,3},{4,12},{12,4},... | collective-permute-start | bytes 638984 | tf_op jit(solution)/shard_map/ppermute | solution.py:280
  14.6 3.7 %collective-permute-start.2 = (f32[85,8,128]{2,1,0:T(8,128)S(1)}, f32[85,8,128]{2,1,0:T(8,128)S(1)}, u32[]{:S(2)}, u32[]{:S(2)}) collective-permute-start(f32[85,8,128]{2,1,0:T(8,128)S(1)} %get-tuple-element.16), channel_id=1, source_target_pairs={{1,2},{2,1},{3,4},{4,3},{5,6},{6,5},{9,10},{10,9},{11,12},{12,11},... | collective-permute-start | bytes 1044488 | tf_op jit(solution)/shard_map/ppermute | solution.py:280
  15.3 11.2 %collective-permute-start.3 = (f32[85,8,128]{2,1,0:T(8,128)S(1)}, f32[85,8,128]{2,1,0:T(8,128)S(1)}, u32[]{:S(2)}, u32[]{:S(2)}) collective-permute-start(f32[85,8,128]{2,1,0:T(8,128)S(1)} %get-tuple-element.17), channel_id=1, source_target_pairs={{0,1},{1,0},{2,3},{3,2},{4,5},{5,4},{6,7},{7,6},{8,9},{9,8},{10,11... | collective-permute-start | bytes 1044488 | tf_op jit(solution)/shard_map/ppermute | solution.py:280

commit v3 on v2

--- a/solution.py
+++ b/solution.py
@@ -16,9 +16,10 @@
 ALPHA = (-COURANT, 1.0)
 BETA = (1.0, -COURANT)
 
-UP_LINES = (("ax", 10), ("ay", 10), ("px", 8), ("py", 8))
-DOWN_LINES = (("sx", 11), ("sy", 10), ("qx", 9), ("qy", 8))
-LINES = 2 * 38 + 9
+UP = (("ax", 10, 1, 1), ("ay", 10, 1, 2), ("px", 8, 1, 1), ("py", 8, 1, 2))
+DOWN = (("sx", 11, 2, 1), ("sy", 10, 1, 1), ("qx", 9, 1, 1), ("qy", 8, 1, 1))
+EARLY = 2 * 29 + 8
+LATE = 2 * 10 + 1
 HALO = 26
 
 
@@ -70,34 +71,73 @@
     return jnp.where(first, 0.0, 1.0).astype(jnp.float32)
 
 
-def pack_kernel(eps_ref, e, h, g, k, m, pair_ref, next_ref, eps, strips, kinds, sems):
-    copies = [pltpu.make_async_copy(eps_ref, eps, sems.at[10])]
-    for side, start in enumerate((0, 6)):
-        for field, ref in enumerate((e, h, g, k)):
-            copies.append(
-                pltpu.make_async_copy(ref.at[:, start : start + 2], strips.at[side, field], sems.at[side * 5 + field])
-            )
-        copies.append(pltpu.make_async_copy(m.at[start : start + 2], kinds.at[side], sems.at[side * 5 + 4]))
+def pack_kernel(eps_ref, e, h, g, k, m, pair_ref, next_ref, early0, early1, eps, fields, kinds, sems):
+    copies = [pltpu.make_async_copy(eps_ref, eps, sems.at[5]), pltpu.make_async_copy(m, kinds, sems.at[4])]
+    for field, ref in enumerate((e, h, g, k)):
+        copies.append(pltpu.make_async_copy(ref, fields.at[field], sems.at[field]))
     for copy in copies:
         copy.start()
     for copy in copies:
         copy.wait()
     even = lax.axis_index("c") == 0
+    even_z = lax.axis_index("x") % 2 == 0
     values = coefs(eps)
 
-    def put(row, first, last):
-        pair_ref[row] = jnp.where(even, last, first)
-        next_ref[row] = jnp.where(even, first, last)
+    coef = [table(kinds[:, plane(z), :], values) for z in range(2)]
+    row = 0
+    for chain in range(2):
+        alpha, beta = ALPHA[chain], BETA[chain]
+
+        def load(field, comp, z):
+            return fields[field, comp, :, plane(z), :]
+
+        s = [[load(2 * chain, comp, z) for z in range(2)] for comp in range(3)]
+        if chain == 1:
+            s = [[s[comp][z] * coef[z] for z in range(2)] for comp in range(3)]
+        sx, sy, sz = s
+        tx, ty, tz = [], [], []
+        for z in range(2):
+            dz_y = sy[1] - sy[0] if z == 0 else -sy[1]
+            dz_x = sx[1] - sx[0] if z == 0 else -sx[1]
+            tx.append(load(2 * chain + 1, 0, z) + alpha * (ahead_y(sz[z]) - dz_y))
+            ty.append(load(2 * chain + 1, 1, z)[:7] + alpha * (dz_x[:7] - (sz[z][1:] - sz[z][:7])))
+            tz.append(load(2 * chain + 1, 2, z)[:7] + alpha * ((sy[z][1:] - sy[z][:7]) - ahead_y(sx[z][:7])))
+        b0, b1 = beta * coef[0], beta * coef[1]
+        qx = sx[0][:7] + b0[:7] * (behind_y(tz[0]) - ty[0])
+        qy = sy[0][1:7] + b0[1:7] * (tx[0][1:7] - (tz[0][1:] - tz[0][:6]))
+        s1x = sx[1][:7] + b1[:7] * (behind_y(tz[1]) - (ty[1] - ty[0]))
+        s1y = sy[1][1:7] + b1[1:7] * ((tx[1] - tx[0])[1:7] - (tz[1][1:] - tz[1][:6]))
+        s1z = sz[1][1:7] + b1[1:7] * ((ty[1][1:] - ty[1][:6]) - behind_y(tx[1][1:7]))
+        px = tx[1][1:7] + alpha * (ahead_y(s1z) + s1y)
+        py = ty[1][1:6] - alpha * (s1x[1:6] + (s1z[1:] - s1z[:5]))
+        up = jnp.concatenate([tx[1], ty[1], px, py, jnp.zeros((3, 8, 128), jnp.float32)], axis=0)
+        down = jnp.concatenate([sx[0], sy[0], qx, qy], axis=0)
+        early0[pl.ds(row, 29)] = jnp.where(even_z, up, down)
+        early1[pl.ds(row, 29)] = jnp.where(even_z, down, up)
+        row += 29
+    early0[pl.ds(row, 8)] = jnp.where(even_z, coef[1], coef[0])
+    early1[pl.ds(row, 8)] = jnp.where(even_z, coef[0], coef[1])
+
+    def put(line, first, last):
+        pair_ref[line] = jnp.where(even, last, first)
+        next_ref[line] = jnp.where(even, first, last)
 
     for field in range(4):
         for comp in range(3):
             for line in range(2):
-                put(field * 6 + comp * 2 + line, strips[0, field, comp, line], strips[1, field, comp, line])
+                put(field * 6 + comp * 2 + line, fields[field, comp, line], fields[field, comp, 6 + line])
     for line in range(2):
-        put(24 + line, table(kinds[0, line], values), table(kinds[1, line], values))
-
-
-def local_kernel(eps_ref, e, h, g, kf, m, next_ref, pair_ref, pay0, pay1, t1s, s1s, s0s, cs):
+        put(24 + line, table(kinds[line], values), table(kinds[6 + line], values))
+
+
+def edges(planes, layout):
+    picked = []
+    for value, (_, count, low, high) in zip(planes, layout):
+        picked += [value[:low], value[count - high :]]
+    return jnp.concatenate(picked, axis=0)
+
+
+def local_kernel(eps_ref, e, h, g, kf, m, next_ref, pair_ref, late0, late1, t1s, s1s, s0s, cs):
     even_x = lax.axis_index("c") == 0
     even_z = lax.axis_index("x") % 2 == 0
     x_flag = low_flag(XY)
@@ -121,10 +161,6 @@
         own = table(m[:, plane(z), :], values)
         coef.append(jnp.concatenate([below(24, z), below(25, z), own, above(24, z), above(25, z)], axis=0))
         cs[z] = coef[z][1:11]
-
-    def put(row, up, down):
-        pay0[row] = jnp.where(even_z, up, down)
-        pay1[row] = jnp.where(even_z, down, up)
 
     for chain in range(2):
         alpha, beta = ALPHA[chain], BETA[chain]
@@ -161,32 +197,43 @@
         ax, ay = t1[0][1][1:], t1[1][1][1:]
         px = ax[1:9] + alpha * (ahead_y(s1[2][1][1:9]) + s1[1][1][1:9])
         py = ay[1:9] - alpha * (s1[0][1][1:9] + (s1[2][1][2:10] - s1[2][1][1:9]))
-        up = jnp.concatenate([ax, ay, px, py, jnp.zeros((2, 8, 128), jnp.float32)], axis=0)
-        down = jnp.concatenate([sx[0][:11], sy[0][1:11], s1[0][0][:9], s1[1][0][1:9]], axis=0)
-        put(pl.ds(38 * chain, 38), up, down)
-    put(pl.ds(76, 9), coef[1][2:11], coef[0][1:10])
-
-
-def final_kernel(eps_ref, e, g, m, owner, r1, r0, t1s, s1s, s0s, cs, adj_e, adj_h, sums):
+        up = (ax, ay, px, py)
+        down = (sx[0][:11], sy[0][1:11], s1[0][0][:9], s1[1][0][1:9])
+        late_up = edges(up, UP)
+        late_down = jnp.concatenate([edges(down, DOWN), jnp.zeros((1, 8, 128), jnp.float32)], axis=0)
+        late0[pl.ds(10 * chain, 10)] = jnp.where(even_z, late_up, late_down)
+        late1[pl.ds(10 * chain, 10)] = jnp.where(even_z, late_down, late_up)
+    late0[20] = jnp.where(even_z, coef[1][10], coef[0][1])
+    late1[20] = jnp.where(even_z, coef[0][1], coef[1][10])
+
+
+def final_kernel(eps_ref, e, g, m, owner, early1, early0, late1, late0, t1s, s1s, s0s, cs, adj_e, adj_h, sums):
     even_z = lax.axis_index("x") % 2 == 0
     x_flag, z_flag = low_flag(XY), low_flag(GZ)
     values = coefs(eps_ref)
     inverse = [2.0 * eps_ref[kind] for kind in range(4)]
 
-    def above(start, count):
-        return jnp.where(even_z, r0[pl.ds(start, count)], r1[pl.ds(start, count)])
-
-    def below(start, count):
-        return jnp.where(even_z, r1[pl.ds(start, count)], r0[pl.ds(start, count)])
-
-    c_up, c_low = above(76, 9), below(76, 9)
+    def joined(early_lines, late_lines, layout, chain, at):
+        first, edge = 29 * chain, 10 * chain
+        for _, count, low, high in layout[:at]:
+            first, edge = first + count - low - high, edge + low + high
+        _, count, low, high = layout[at]
+        middle = early_lines(first, count - low - high)
+        return jnp.concatenate([late_lines(edge, low), middle, late_lines(edge + low, high)], axis=0)
+
+    def select(if_even, if_odd):
+        return lambda start, count: jnp.where(even_z, if_even[pl.ds(start, count)], if_odd[pl.ds(start, count)])
+
+    early_up, late_up = select(early0, early1), select(late0, late1)
+    early_low, late_low = select(early1, early0), select(late1, late0)
+    c_up = jnp.concatenate([late_up(20, 1), early_up(58, 8)], axis=0)
+    c_low = jnp.concatenate([early_low(58, 8), late_low(20, 1)], axis=0)
     own = slice(1, 9)
     kept = []
     for chain in range(2):
         alpha, beta = ALPHA[chain], BETA[chain]
-        base = 38 * chain
-        sx2, sy2, qx, qy = above(base, 11), above(base + 11, 10), above(base + 21, 9), above(base + 30, 8)
-        ax, ay, px, py = below(base, 10), below(base + 10, 10), below(base + 20, 8), below(base + 28, 8)
+        sx2, sy2, qx, qy = (joined(early_up, late_up, DOWN, chain, at) for at in range(4))
+        ax, ay, px, py = (joined(early_low, late_low, UP, chain, at) for at in range(4))
         sx0, sy0 = s0s[chain, 0], s0s[chain, 1]
         tx = [t1s[chain, 0, 0][1:], t1s[chain, 0, 1][1:] - alpha * sy2]
         ty = [t1s[chain, 1, 0][1:], t1s[chain, 1, 1][1:] + alpha * sx2[1:]]
@@ -288,27 +335,29 @@
 
 def body(e_check, h_check, adj_e, adj_h, material, owner, permittivity):
     e, h, g, k, m, own = (rows(u) for u in (e_check, h_check, adj_e, adj_h, material, owner))
-    pair, following = pl.pallas_call(
+    pair, following, early0, early1 = pl.pallas_call(
         pack_kernel,
-        out_shape=(f32(HALO, 16, 128), f32(HALO, 16, 128)),
+        out_shape=(f32(HALO, 16, 128), f32(HALO, 16, 128), f32(EARLY, 8, 128), f32(EARLY, 8, 128)),
         in_specs=[HBM] * 6,
-        out_specs=[VMEM] * 2,
+        out_specs=[VMEM] * 4,
         scratch_shapes=[
             pltpu.SMEM((4,), jnp.float32),
-            pltpu.VMEM((2, 4, 3, 2, 16, 128), jnp.float32),
-            pltpu.VMEM((2, 2, 16, 128), jnp.int32),
-            pltpu.SemaphoreType.DMA((11,)),
+            pltpu.VMEM((4, 3, 8, 16, 128), jnp.float32),
+            pltpu.VMEM((8, 16, 128), jnp.int32),
+            pltpu.SemaphoreType.DMA((6,)),
         ],
         compiler_params=pltpu.CompilerParams(vmem_limit_bytes=LARGE),
         name="pack",
     )(permittivity, e, h, g, k, m)
+    early1 = swap_pairs(early1, GZ, 1)
+    early0 = swap_pairs(early0, "x", 0)
     pair = swap_pairs(pair, "c", 0)
     following = swap_pairs(following, XY, 1)
-    pay0, pay1, t1s, s1s, s0s, cs = pl.pallas_call(
+    late0, late1, t1s, s1s, s0s, cs = pl.pallas_call(
         local_kernel,
         out_shape=(
-            f32(LINES, 8, 128),
-            f32(LINES, 8, 128),
+            f32(LATE, 8, 128),
+            f32(LATE, 8, 128),
             f32(2, 3, 2, 11, 8, 128),
             f32(2, 3, 2, 10, 8, 128),
             f32(2, 2, 10, 8, 128),
@@ -317,18 +366,19 @@
         in_specs=[SMEM] + [VMEM] * 7,
         out_specs=[VMEM] * 6,
         compiler_params=PARAMS,
+        cost_estimate=pl.CostEstimate(flops=1, bytes_accessed=1, transcendentals=0),
         name="local_step",
     )(permittivity, e, h, g, k, m, following, pair)
-    pay0 = swap_pairs(pay0, "x", 0)
-    pay1 = swap_pairs(pay1, GZ, 1)
+    late1 = swap_pairs(late1, GZ, 1)
+    late0 = swap_pairs(late0, "x", 0)
     out_e, out_h, sums = pl.pallas_call(
         final_kernel,
         out_shape=(f32(3, 8, 16, 128), f32(3, 8, 16, 128), f32(1, 128)),
-        in_specs=[SMEM] + [VMEM] * 10,
+        in_specs=[SMEM] + [VMEM] * 12,
         out_specs=[VMEM] * 3,
         compiler_params=PARAMS,
         name="final_step",
-    )(permittivity, e, g, m, own, pay1, pay0, t1s, s1s, s0s, cs)
+    )(permittivity, e, g, m, own, early1, early0, late1, late0, t1s, s1s, s0s, cs)
     total = spread_sum(sums[0], ("zl", "zh", "c"))
     total = spread_sum(total, ("y", "x"))
     cells = 8 * lax.axis_size(XY) * 2 * lax.axis_size(GZ) * 1024

time: 73.6 us -> 71 us (0.965)
  starting transfers between devices: 13.3 us -> 26.3 us
  blocking collectives: 44.3 us -> 35.6 us
  waiting for transfers between devices: 9.47 us -> 1.84 us
    ppermute x4 -> x6, starting transfers between devices: 13.3 us -> 26.3 us  [swap_pairs(): return lax.ppermute(value, axes, pairs)]
    all_to_all x2, blocking collectives: 44.3 us -> 35.6 us  [spread_sum(): return jnp.sum(lax.all_to_all(sent, axes, 0, 0), axis=0)]
    ppermute x4 -> x6, waiting for transfers between devices: 9.47 us -> 1.84 us  [swap_pairs(): return lax.ppermute(value, axes, pairs)]
  transfers between devices with their start and end apart: 4 -> 6, of which waited for: 2 -> 1; matrix products, arithmetic and copies ran while one was open for 0% -> 0% of each run, Pallas kernels for 0% -> 1%
where the time goes in v3:
time: 71 us; the launch traced here: 70.6 us
  blocking collectives  35.6 us (50%)
  starting transfers between devices  26.3 us (37%)
  Pallas kernels  5.46 us (8%)
  waiting for transfers between devices  1.84 us (3%)
  between operations  0.84 us (1%)
    all_to_all x2, blocking collectives, spread_sum(): return jnp.sum(lax.all_to_all(sent, axes, 0, 0), axis=0)  35.6 us
    ppermute x6, starting transfers between devices, swap_pairs(): return lax.ppermute(value, axes, pairs)  26.3 us
    pallas_call x1, Pallas kernels, body(): pl.pallas_call(pack_kernel, out_shape=(f32(HALO, 16, 128), f32(HALO, 16,...  2.62 us
    pallas_call x1, Pallas kernels, body(): pl.pallas_call(final_kernel, out_shape=(f32(3, 8, 16, 128), f32(3, 8, 16,...  1.88 us
    ppermute x6, waiting for transfers between devices, swap_pairs(): return lax.ppermute(value, axes, pairs)  1.84 us
  transfers between devices with their start and end apart: 6, of which 1 were waited for; matrix products, arithmetic and copies ran while one was open for 0% of the time, Pallas kernels for 1%

profile of v3, /device:TPU:1, one launch (start us, length us, event | category | flops | bytes accessed | tf_op | source)
XLA Modules:
  0.0 70.6 jit_solution(2299179679029831801)
XLA Ops:
  0.6 0.0 copy-start
  0.6 0.0 copy-start.1
  0.7 0.0 copy-start.2
  0.7 0.0 copy-start.3
  0.7 0.0 copy-start.4
  0.7 2.6 %pack.1 = (f32[26,16,128]{2,1,0:T(8,128)}, f32[26,16,128]{2,1,0:T(8,128)}, f32[66,8,128]{2,1,0:T(8,128)}, f32[66,8,128]{2,1,0:T(8,128)}) custom-call(f32[4]{0:T(128)} %eps_ref.5, f32[3,8,16,128]{3,2,1,0:T(8,128)} %bitcast.43, f32[3,8,16,128]{3,2,1,0:T(8,128)} %bitcast.49, f32[3,8,16,128]{3,2,1,0:T(8,128)} %bitcast.46, f32[3,8,16,128]{3,2,1,0:T(8,128)} %bitcast.51, ...), custom_call_target="tpu_custom_call" | custom-call | tf_op jit(solution)/shard_map/pack/pallas_call | solution.py:338
  3.3 4.6 %collective-permute-start.2 = (f32[26,16,128]{2,1,0:T(8,128)}, f32[26,16,128]{2,1,0:T(8,128)S(1)}, u32[]{:S(2)}, u32[]{:S(2)}) collective-permute-start(f32[26,16,128]{2,1,0:T(8,128)} %get-tuple-element.18), channel_id=1, source_target_pairs={{8,16},{16,8},{24,32},{32,24},{40,48},{48,40},{56,64},{64,56},{72,... | collective-permute-start | bytes 638984 | tf_op jit(solution)/shard_map/ppermute | solution.py:327
  7.9 4.9 %collective-permute-start.3 = (f32[26,16,128]{2,1,0:T(8,128)}, f32[26,16,128]{2,1,0:T(8,128)S(1)}, u32[]{:S(2)}, u32[]{:S(2)}) collective-permute-start(f32[26,16,128]{2,1,0:T(8,128)} %get-tuple-element.19), channel_id=1, source_target_pairs={{0,8},{8,0},{1,9},{9,1},{2,10},{10,2},{3,11},{11,3},{4,12},{12,4},... | collective-permute-start | bytes 638984 | tf_op jit(solution)/shard_map/ppermute | solution.py:327
  12.8 0.0 copy-start.6
  12.8 0.7 collective-permute-start
  13.5 0.0 copy-start.5
  13.5 2.7 %collective-permute-start.1 = (f32[66,8,128]{2,1,0:T(8,128)}, f32[66,8,128]{2,1,0:T(8,128)S(1)}, u32[]{:S(2)}, u32[]{:S(2)}) collective-permute-start(f32[66,8,128]{2,1,0:T(8,128)} %get-tuple-element.17), channel_id=1, source_target_pairs={{0,1},{1,0},{2,3},{3,2},{4,5},{5,4},{6,7},{7,6},{8,9},{9,8},{10,11... | collective-permute-start | bytes 811016 | tf_op jit(solution)/shard_map/ppermute | solution.py:327
  16.2 0.0 collective-permute-done.2.next_ref
  16.3 0.0 collective-permute-done.3.pair_ref
  16.3 0.0 copy-done
  16.3 0.0 copy-done.1
  16.3 0.0 copy-done.2
  16.3 0.0 copy-done.3
  16.3 0.0 copy-done.4
  16.3 0.0 copy-done.6
  16.3 1.0 %local_step.1 = (f32[21,8,128]{2,1,0:T(8,128)S(1)}, f32[21,8,128]{2,1,0:T(8,128)S(1)}, f32[2,3,2,11,8,128]{5,4,3,2,1,0:T(8,128)S(1)}, f32[2,3,2,10,8,128]{5,4,3,...) custom-call(f32[4]{0:T(128)S(1)} %copy-done.6, f32[3,8,16,128]{3,2,1,0:T(8,128)S(1)} %bitcast.44, ...), custom_call_target="tpu_custom_call" | custom-call | flops 1 | bytes 1 | tf_op jit(solution)/shard_map/local_step/pallas_call | solution.py:356
  17.3 0.7 collective-permute-start.4
  18.0 12.7 %collective-permute-start.5 = (f32[21,8,128]{2,1,0:T(8,128)S(1)}, f32[21,8,128]{2,1,0:T(8,128)S(1)}, u32[]{:S(2)}, u32[]{:S(2)}) collective-permute-start(f32[21,8,128]{2,1,0:T(8,128)S(1)} %get-tuple-element.21), channel_id=1, source_target_pairs={{0,1},{1,0},{2,3},{3,2},{4,5},{5,4},{6,7},{7,6},{8,9},{9,8},{10,11... | collective-permute-start | bytes 258056 | tf_op jit(solution)/shard_map/ppermute | solution.py:327
  30.7 0.0 collective-permute-done.early1
  30.7 0.0 collective-permute-done.1.early0
  30.7 0.0 collective-permute-done.4.late1
  30.7 1.8 %collective-permute-done.5.late0 = f32[21,8,128]{2,1,0:T(8,128)S(1)} collective-permute-done((f32[21,8,128]{2,1,0:T(8,128)S(1)}, f32[21,8,128]{2,1,0:T(8,128)S(1)}, u32[]{:S(2)}, u32[]{:S(2)}) %collective-permute-start.5) | collective-permute-done | bytes 86048 | tf_op jit(solution)/shard_map/ppermute | solution.py:327
  32.5 0.0 copy-done.5
  32.6 1.9 %final_step.1 = (f32[3,8,16,128]{3,2,1,0:T(8,128)}, f32[3,8,16,128]{3,2,1,0:T(8,128)}, f32[1,128]{1,0:T(1,128)S(1)}) custom-call(f32[4]{0:T(128)S(1)} %copy-done.6, f32[3,8,16,128]{3,2,1,0:T(8,128)S(1)} %bitcast.45, f32[3,8,16,128]{3,2,1,0:T(8,128)S(1)} %bitcast.48, s32[8,16,128]{2,1,0:T(8,128)S(1)} %bitcast.55, s32[8,16,128]{2,1,0:T(8,128)S(1)} %bitcast.56, ...), custom_call_target="tpu_custom_call" | custom-call | tf_op jit(solution)/shard_map/final_step/pallas_call | solution.py:374
  34.4 22.6 %all_to_all.12 = f32[16,1,128]{2,1,0:T(1,128)S(1)} all-to-all(f32[16,1,128]{2,1,0:T(1,128)S(1)} %broadcast_in_dim.4), channel_id=1, replica_groups=mesh['zl'=4,'y'=8,'c'=2,'zh'=2,'x'=4] {'zl','zh','c'}, dimensions={0} | all-to-all | bytes 16384 | tf_op jit(solution)/shard_map/all_to_all | solution.py:333
  57.1 13.0 %all_to_all.13 = f32[32,1,128]{2,1,0:T(1,128)S(1)} all-to-all(f32[32,1,128]{2,1,0:T(1,128)S(1)} %broadcast_in_dim.5), channel_id=1, replica_groups=mesh['zl'=4,'y'=8,'c'=2,'zh'=2,'x'=4] {'y','x'}, dimensions={0} | all-to-all | bytes 32768 | tf_op jit(solution)/shard_map/all_to_all | solution.py:333
  70.1 0.5 slice_multiply_fusion
  (4 shorter events, 0.1 us)
Async XLA Ops:
  0.6 15.6 %copy-start = (f32[3,8,2,1024]{3,2,1,0:T(2,128)S(1)}, f32[3,8,2,1024]{3,2,1,0:T(2,128)}, u32[]{:S(2)}) copy-start(f32[3,8,2,1024]{3,2,1,0:T(2,128)} %param.7) | copy-start | bytes 589828
  0.6 15.6 %copy-start.1 = (f32[3,8,2,1024]{3,2,1,0:T(2,128)S(1)}, f32[3,8,2,1024]{3,2,1,0:T(2,128)}, u32[]{:S(2)}) copy-start(f32[3,8,2,1024]{3,2,1,0:T(2,128)} %param.9) | copy-start | bytes 589828
  0.7 15.6 %copy-start.2 = (f32[3,8,2,1024]{3,2,1,0:T(2,128)S(1)}, f32[3,8,2,1024]{3,2,1,0:T(2,128)}, u32[]{:S(2)}) copy-start(f32[3,8,2,1024]{3,2,1,0:T(2,128)} %param.8) | copy-start | bytes 589828
  0.7 15.6 %copy-start.3 = (f32[3,8,2,1024]{3,2,1,0:T(2,128)S(1)}, f32[3,8,2,1024]{3,2,1,0:T(2,128)}, u32[]{:S(2)}) copy-start(f32[3,8,2,1024]{3,2,1,0:T(2,128)} %param.10) | copy-start | bytes 589828
  0.7 15.6 %copy-start.4 = (s32[8,2,1024]{2,1,0:T(2,128)S(1)}, s32[8,2,1024]{2,1,0:T(2,128)}, u32[]{:S(2)}) copy-start(s32[8,2,1024]{2,1,0:T(2,128)} %param.11) | copy-start | bytes 196612
  3.3 12.9 %collective-permute-start.2 = (f32[26,16,128]{2,1,0:T(8,128)}, f32[26,16,128]{2,1,0:T(8,128)S(1)}, u32[]{:S(2)}, u32[]{:S(2)}) collective-permute-start(f32[26,16,128]{2,1,0:T(8,128)} %get-tuple-element.18), channel_id=1, source_target_pairs={{8,16},{16,8},{24,32},{32,24},{40,48},{48,40},{56,64},{64,56},{72,... | collective-permute-start | bytes 638984 | tf_op jit(solution)/shard_map/ppermute | solution.py:327
  7.9 8.4 %collective-permute-start.3 = (f32[26,16,128]{2,1,0:T(8,128)}, f32[26,16,128]{2,1,0:T(8,128)S(1)}, u32[]{:S(2)}, u32[]{:S(2)}) collective-permute-start(f32[26,16,128]{2,1,0:T(8,128)} %get-tuple-element.19), channel_id=1, source_target_pairs={{0,8},{8,0},{1,9},{9,1},{2,10},{10,2},{3,11},{11,3},{4,12},{12,4},... | collective-permute-start | bytes 638984 | tf_op jit(solution)/shard_map/ppermute | solution.py:327
  12.8 3.5 %copy-start.6 = (f32[4]{0:T(128)S(1)}, f32[4]{0:T(128)}, u32[]{:S(2)}) copy-start(f32[4]{0:T(128)} %eps_ref.5) | copy-start | bytes 52
  12.8 17.9 %collective-permute-start = (f32[66,8,128]{2,1,0:T(8,128)}, f32[66,8,128]{2,1,0:T(8,128)S(1)}, u32[]{:S(2)}, u32[]{:S(2)}) collective-permute-start(f32[66,8,128]{2,1,0:T(8,128)} %get-tuple-element.16), channel_id=1, source_target_pairs={{1,2},{2,1},{3,4},{4,3},{5,6},{6,5},{9,10},{10,9},{11,12},{12,11},... | collective-permute-start | bytes 811016 | tf_op jit(solution)/shard_map/ppermute | solution.py:327
  13.5 19.1 %copy-start.5 = (s32[8,2,1024]{2,1,0:T(2,128)S(1)}, s32[8,2,1024]{2,1,0:T(2,128)}, u32[]{:S(2)}) copy-start(s32[8,2,1024]{2,1,0:T(2,128)} %param.12) | copy-start | bytes 196612
  13.5 17.2 %collective-permute-start.1 = (f32[66,8,128]{2,1,0:T(8,128)}, f32[66,8,128]{2,1,0:T(8,128)S(1)}, u32[]{:S(2)}, u32[]{:S(2)}) collective-permute-start(f32[66,8,128]{2,1,0:T(8,128)} %get-tuple-element.17), channel_id=1, source_target_pairs={{0,1},{1,0},{2,3},{3,2},{4,5},{5,4},{6,7},{7,6},{8,9},{9,8},{10,11... | collective-permute-start | bytes 811016 | tf_op jit(solution)/shard_map/ppermute | solution.py:327
  17.3 13.4 %collective-permute-start.4 = (f32[21,8,128]{2,1,0:T(8,128)S(1)}, f32[21,8,128]{2,1,0:T(8,128)S(1)}, u32[]{:S(2)}, u32[]{:S(2)}) collective-permute-start(f32[21,8,128]{2,1,0:T(8,128)S(1)} %get-tuple-element.20), channel_id=1, source_target_pairs={{1,2},{2,1},{3,4},{4,3},{5,6},{6,5},{9,10},{10,9},{11,12},{12,11},... | collective-permute-start | bytes 258056 | tf_op jit(solution)/shard_map/ppermute | solution.py:327
  18.0 14.6 %collective-permute-start.5 = (f32[21,8,128]{2,1,0:T(8,128)S(1)}, f32[21,8,128]{2,1,0:T(8,128)S(1)}, u32[]{:S(2)}, u32[]{:S(2)}) collective-permute-start(f32[21,8,128]{2,1,0:T(8,128)S(1)} %get-tuple-element.21), channel_id=1, source_target_pairs={{0,1},{1,0},{2,3},{3,2},{4,5},{5,4},{6,7},{7,6},{8,9},{9,8},{10,11... | collective-permute-start | bytes 258056 | tf_op jit(solution)/shard_map/ppermute | solution.py:327

commit v4 on v3

--- a/solution.py
+++ b/solution.py
@@ -18,6 +18,7 @@
 
 UP = (("ax", 10, 1, 1), ("ay", 10, 1, 2), ("px", 8, 1, 1), ("py", 8, 1, 2))
 DOWN = (("sx", 11, 2, 1), ("sy", 10, 1, 1), ("qx", 9, 1, 1), ("qy", 8, 1, 1))
+LINES = 2 * 38 + 9
 EARLY = 2 * 29 + 8
 LATE = 2 * 10 + 1
 HALO = 26
@@ -71,7 +72,7 @@
     return jnp.where(first, 0.0, 1.0).astype(jnp.float32)
 
 
-def pack_kernel(eps_ref, e, h, g, k, m, pair_ref, next_ref, early0, early1, eps, fields, kinds, sems):
+def pack_kernel(eps_ref, e, h, g, k, m, pair_ref, next_ref, early, eps, fields, kinds, sems):
     copies = [pltpu.make_async_copy(eps_ref, eps, sems.at[5]), pltpu.make_async_copy(m, kinds, sems.at[4])]
     for field, ref in enumerate((e, h, g, k)):
         copies.append(pltpu.make_async_copy(ref, fields.at[field], sems.at[field]))
@@ -112,11 +113,9 @@
         py = ty[1][1:6] - alpha * (s1x[1:6] + (s1z[1:] - s1z[:5]))
         up = jnp.concatenate([tx[1], ty[1], px, py, jnp.zeros((3, 8, 128), jnp.float32)], axis=0)
         down = jnp.concatenate([sx[0], sy[0], qx, qy], axis=0)
-        early0[pl.ds(row, 29)] = jnp.where(even_z, up, down)
-        early1[pl.ds(row, 29)] = jnp.where(even_z, down, up)
+        early[pl.ds(row, 29)] = jnp.where(even_z, down, up)
         row += 29
-    early0[pl.ds(row, 8)] = jnp.where(even_z, coef[1], coef[0])
-    early1[pl.ds(row, 8)] = jnp.where(even_z, coef[0], coef[1])
+    early[pl.ds(row, 8)] = jnp.where(even_z, coef[0], coef[1])
 
     def put(line, first, last):
         pair_ref[line] = jnp.where(even, last, first)
@@ -137,7 +136,7 @@
     return jnp.concatenate(picked, axis=0)
 
 
-def local_kernel(eps_ref, e, h, g, kf, m, next_ref, pair_ref, late0, late1, t1s, s1s, s0s, cs):
+def local_kernel(eps_ref, e, h, g, kf, m, next_ref, pair_ref, pay0, late, t1s, s1s, s0s, cs):
     even_x = lax.axis_index("c") == 0
     even_z = lax.axis_index("x") % 2 == 0
     x_flag = low_flag(XY)
@@ -199,41 +198,51 @@
         py = ay[1:9] - alpha * (s1[0][1][1:9] + (s1[2][1][2:10] - s1[2][1][1:9]))
         up = (ax, ay, px, py)
         down = (sx[0][:11], sy[0][1:11], s1[0][0][:9], s1[1][0][1:9])
-        late_up = edges(up, UP)
+        full_up = jnp.concatenate([*up, jnp.zeros((2, 8, 128), jnp.float32)], axis=0)
+        pay0[pl.ds(38 * chain, 38)] = jnp.where(even_z, full_up, jnp.concatenate(down, axis=0))
         late_down = jnp.concatenate([edges(down, DOWN), jnp.zeros((1, 8, 128), jnp.float32)], axis=0)
-        late0[pl.ds(10 * chain, 10)] = jnp.where(even_z, late_up, late_down)
-        late1[pl.ds(10 * chain, 10)] = jnp.where(even_z, late_down, late_up)
-    late0[20] = jnp.where(even_z, coef[1][10], coef[0][1])
-    late1[20] = jnp.where(even_z, coef[0][1], coef[1][10])
-
-
-def final_kernel(eps_ref, e, g, m, owner, early1, early0, late1, late0, t1s, s1s, s0s, cs, adj_e, adj_h, sums):
+        late[pl.ds(10 * chain, 10)] = jnp.where(even_z, late_down, edges(up, UP))
+    pay0[pl.ds(76, 9)] = jnp.where(even_z, coef[1][2:11], coef[0][1:10])
+    late[20] = jnp.where(even_z, coef[0][1], coef[1][10])
+
+
+def take_kernel(early, taken):
+    del early, taken
+
+
+def final_kernel(eps_ref, e, g, m, owner, early, late, r0, t1s, s1s, s0s, cs, adj_e, adj_h, sums):
     even_z = lax.axis_index("x") % 2 == 0
     x_flag, z_flag = low_flag(XY), low_flag(GZ)
     values = coefs(eps_ref)
     inverse = [2.0 * eps_ref[kind] for kind in range(4)]
 
-    def joined(early_lines, late_lines, layout, chain, at):
+    def odd_pair(layout, chain, at):
         first, edge = 29 * chain, 10 * chain
         for _, count, low, high in layout[:at]:
             first, edge = first + count - low - high, edge + low + high
         _, count, low, high = layout[at]
-        middle = early_lines(first, count - low - high)
-        return jnp.concatenate([late_lines(edge, low), middle, late_lines(edge + low, high)], axis=0)
-
-    def select(if_even, if_odd):
-        return lambda start, count: jnp.where(even_z, if_even[pl.ds(start, count)], if_odd[pl.ds(start, count)])
-
-    early_up, late_up = select(early0, early1), select(late0, late1)
-    early_low, late_low = select(early1, early0), select(late1, late0)
-    c_up = jnp.concatenate([late_up(20, 1), early_up(58, 8)], axis=0)
-    c_low = jnp.concatenate([early_low(58, 8), late_low(20, 1)], axis=0)
+        middle = early[pl.ds(first, count - low - high)]
+        return jnp.concatenate([late[pl.ds(edge, low)], middle, late[pl.ds(edge + low, high)]], axis=0)
+
+    def even_pair(layout, chain, at):
+        start = 38 * chain + sum(count for _, count, _, _ in layout[:at])
+        return r0[pl.ds(start, layout[at][1])]
+
+    def above(chain, at):
+        return jnp.where(even_z, even_pair(DOWN, chain, at), odd_pair(DOWN, chain, at))
+
+    def below(chain, at):
+        return jnp.where(even_z, odd_pair(UP, chain, at), even_pair(UP, chain, at))
+
+    edge, body_lines, full = late[pl.ds(20, 1)], early[pl.ds(58, 8)], r0[pl.ds(76, 9)]
+    c_up = jnp.where(even_z, full, jnp.concatenate([edge, body_lines], axis=0))
+    c_low = jnp.where(even_z, jnp.concatenate([body_lines, edge], axis=0), full)
     own = slice(1, 9)
     kept = []
     for chain in range(2):
         alpha, beta = ALPHA[chain], BETA[chain]
-        sx2, sy2, qx, qy = (joined(early_up, late_up, DOWN, chain, at) for at in range(4))
-        ax, ay, px, py = (joined(early_low, late_low, UP, chain, at) for at in range(4))
+        sx2, sy2, qx, qy = (above(chain, at) for at in range(4))
+        ax, ay, px, py = (below(chain, at) for at in range(4))
         sx0, sy0 = s0s[chain, 0], s0s[chain, 1]
         tx = [t1s[chain, 0, 0][1:], t1s[chain, 0, 1][1:] - alpha * sy2]
         ty = [t1s[chain, 1, 0][1:], t1s[chain, 1, 1][1:] + alpha * sx2[1:]]
@@ -298,7 +307,9 @@
 
 VMEM = pl.BlockSpec(memory_space=pltpu.VMEM)
 SMEM = pl.BlockSpec(memory_space=pltpu.SMEM)
+ANY = pl.BlockSpec(memory_space=pl.ANY)
 HBM = pl.BlockSpec(memory_space=pltpu.HBM)
+TAKE = 2 * 10**10
 LARGE = 62 * 1024 * 1024
 PARAMS = pltpu.CompilerParams(vmem_limit_bytes=48 * 1024 * 1024)
 
@@ -335,11 +346,11 @@
 
 def body(e_check, h_check, adj_e, adj_h, material, owner, permittivity):
     e, h, g, k, m, own = (rows(u) for u in (e_check, h_check, adj_e, adj_h, material, owner))
-    pair, following, early0, early1 = pl.pallas_call(
+    pair, following, early = pl.pallas_call(
         pack_kernel,
-        out_shape=(f32(HALO, 16, 128), f32(HALO, 16, 128), f32(EARLY, 8, 128), f32(EARLY, 8, 128)),
+        out_shape=(f32(HALO, 16, 128), f32(HALO, 16, 128), f32(EARLY, 8, 128)),
         in_specs=[HBM] * 6,
-        out_specs=[VMEM] * 4,
+        out_specs=[VMEM] * 3,
         scratch_shapes=[
             pltpu.SMEM((4,), jnp.float32),
             pltpu.VMEM((4, 3, 8, 16, 128), jnp.float32),
@@ -349,14 +360,13 @@
         compiler_params=pltpu.CompilerParams(vmem_limit_bytes=LARGE),
         name="pack",
     )(permittivity, e, h, g, k, m)
-    early1 = swap_pairs(early1, GZ, 1)
-    early0 = swap_pairs(early0, "x", 0)
+    early = swap_pairs(early, GZ, 1)
     pair = swap_pairs(pair, "c", 0)
     following = swap_pairs(following, XY, 1)
-    late0, late1, t1s, s1s, s0s, cs = pl.pallas_call(
+    pay0, late, t1s, s1s, s0s, cs = pl.pallas_call(
         local_kernel,
         out_shape=(
-            f32(LATE, 8, 128),
+            f32(LINES, 8, 128),
             f32(LATE, 8, 128),
             f32(2, 3, 2, 11, 8, 128),
             f32(2, 3, 2, 10, 8, 128),
@@ -369,16 +379,26 @@
         cost_estimate=pl.CostEstimate(flops=1, bytes_accessed=1, transcendentals=0),
         name="local_step",
     )(permittivity, e, h, g, k, m, following, pair)
-    late1 = swap_pairs(late1, GZ, 1)
-    late0 = swap_pairs(late0, "x", 0)
+    pay0 = swap_pairs(pay0, "x", 0)
+    late = swap_pairs(late, GZ, 1)
+    early = pl.pallas_call(
+        take_kernel,
+        out_shape=f32(EARLY, 8, 128),
+        in_specs=[ANY],
+        out_specs=ANY,
+        input_output_aliases={0: 0},
+        compiler_params=PARAMS,
+        cost_estimate=pl.CostEstimate(flops=TAKE, bytes_accessed=10**9, transcendentals=0),
+        name="take_early",
+    )(early)
     out_e, out_h, sums = pl.pallas_call(
         final_kernel,
         out_shape=(f32(3, 8, 16, 128), f32(3, 8, 16, 128), f32(1, 128)),
-        in_specs=[SMEM] + [VMEM] * 12,
+        in_specs=[SMEM] + [VMEM] * 11,
         out_specs=[VMEM] * 3,
         compiler_params=PARAMS,
         name="final_step",
-    )(permittivity, e, g, m, own, early1, early0, late1, late0, t1s, s1s, s0s, cs)
+    )(permittivity, e, g, m, own, early, late, pay0, t1s, s1s, s0s, cs)
     total = spread_sum(sums[0], ("zl", "zh", "c"))
     total = spread_sum(total, ("y", "x"))
     cells = 8 * lax.axis_size(XY) * 2 * lax.axis_size(GZ) * 1024

time: 71 us -> 72.2 us (1.017)
  starting transfers between devices: 26.3 us -> 16.2 us
  waiting for transfers between devices: 1.84 us -> 9.81 us
  blocking collectives: 35.6 us -> 39.1 us
    ppermute x6 -> x5, starting transfers between devices: 26.3 us -> 16.2 us  [swap_pairs(): return lax.ppermute(value, axes, pairs)]
    ppermute x6 -> x5, waiting for transfers between devices: 1.84 us -> 9.81 us  [swap_pairs(): return lax.ppermute(value, axes, pairs)]
    all_to_all x2, blocking collectives: 35.6 us -> 39.1 us  [spread_sum(): return jnp.sum(lax.all_to_all(sent, axes, 0, 0), axis=0)]
  transfers between devices with their start and end apart: 6 -> 5, of which waited for: 1 -> 2; matrix products, arithmetic and copies ran while one was open for 0% -> 0% of each run, Pallas kernels for 1% -> 1%
where the time goes in v4:
time: 72.2 us; the launch traced here: 71.8 us
  blocking collectives  39.1 us (54%)
  starting transfers between devices  16.2 us (22%)
  waiting for transfers between devices  9.81 us (14%)
  Pallas kernels  5.37 us (7%)
  between operations  0.79 us (1%)
    all_to_all x2, blocking collectives, spread_sum(): return jnp.sum(lax.all_to_all(sent, axes, 0, 0), axis=0)  39.1 us
    ppermute x5, starting transfers between devices, swap_pairs(): return lax.ppermute(value, axes, pairs)  16.2 us
    ppermute x5, waiting for transfers between devices, swap_pairs(): return lax.ppermute(value, axes, pairs)  9.81 us
    pallas_call x1, Pallas kernels, body(): pl.pallas_call(pack_kernel, out_shape=(f32(HALO, 16, 128), f32(HALO, 16,...  2.52 us
    pallas_call x1, Pallas kernels, body(): pl.pallas_call(final_kernel, out_shape=(f32(3, 8, 16, 128), f32(3, 8, 16,...  1.87 us
  transfers between devices with their start and end apart: 5, of which 2 were waited for; matrix products, arithmetic and copies ran while one was open for 0% of the time, Pallas kernels for 1%

profile of v4, /device:TPU:1, one launch (start us, length us, event | category | flops | bytes accessed | tf_op | source)
XLA Modules:
  0.0 71.8 jit_solution(15732399119273430272)
XLA Ops:
  0.6 0.0 copy-start
  0.6 0.0 copy-start.1
  0.7 0.0 copy-start.2
  0.7 0.0 copy-start.3
  0.7 0.0 copy-start.4
  0.7 2.5 %pack.1 = (f32[26,16,128]{2,1,0:T(8,128)}, f32[26,16,128]{2,1,0:T(8,128)}, f32[66,8,128]{2,1,0:T(8,128)}) custom-call(f32[4]{0:T(128)} %eps_ref.5, f32[3,8,16,128]{3,2,1,0:T(8,128)} %bitcast.43, f32[3,8,16,128]{3,2,1,0:T(8,128)} %bitcast.49, f32[3,8,16,128]{3,2,1,0:T(8,128)} %bitcast.46, f32[3,8,16,128]{3,2,1,0:T(8,128)} %bitcast.51, s32[8,16,128]{2,1,0:T(8,128)} %bitcast.53), custom_call_target="tpu_custom_call" | custom-call | tf_op jit(solution)/shard_map/pack/pallas_call | solution.py:349
  3.2 0.7 collective-permute-start
  3.9 0.0 copy-start.6
  3.9 4.6 %collective-permute-start.1 = (f32[26,16,128]{2,1,0:T(8,128)}, f32[26,16,128]{2,1,0:T(8,128)S(1)}, u32[]{:S(2)}, u32[]{:S(2)}) collective-permute-start(f32[26,16,128]{2,1,0:T(8,128)} %get-tuple-element.16), channel_id=1, source_target_pairs={{8,16},{16,8},{24,32},{32,24},{40,48},{48,40},{56,64},{64,56},{72,... | collective-permute-start | bytes 638984 | tf_op jit(solution)/shard_map/ppermute | solution.py:338
  8.5 4.9 %collective-permute-start.2 = (f32[26,16,128]{2,1,0:T(8,128)}, f32[26,16,128]{2,1,0:T(8,128)S(1)}, u32[]{:S(2)}, u32[]{:S(2)}) collective-permute-start(f32[26,16,128]{2,1,0:T(8,128)} %get-tuple-element.17), channel_id=1, source_target_pairs={{0,8},{8,0},{1,9},{9,1},{2,10},{10,2},{3,11},{11,3},{4,12},{12,4},... | collective-permute-start | bytes 638984 | tf_op jit(solution)/shard_map/ppermute | solution.py:338
  13.4 0.0 collective-permute-done.1.next_ref
  13.4 1.3 %collective-permute-done.2.pair_ref = f32[26,16,128]{2,1,0:T(8,128)S(1)} collective-permute-done((f32[26,16,128]{2,1,0:T(8,128)}, f32[26,16,128]{2,1,0:T(8,128)S(1)}, u32[]{:S(2)}, u32[]{:S(2)}) %collective-permute-start.2) | collective-permute-done | bytes 213024 | tf_op jit(solution)/shard_map/ppermute | solution.py:338
  14.7 0.0 copy-done
  14.7 0.0 copy-done.1
  14.7 0.0 copy-done.2
  14.7 0.0 copy-done.3
  14.7 0.0 copy-done.4
  14.7 0.0 copy-done.6
  14.7 1.0 %local_step.1 = (f32[85,8,128]{2,1,0:T(8,128)S(1)}, f32[21,8,128]{2,1,0:T(8,128)S(1)}, f32[2,3,2,11,8,128]{5,4,3,2,1,0:T(8,128)S(1)}, f32[2,3,2,10,8,128]{5,4,3,...) custom-call(f32[4]{0:T(128)S(1)} %copy-done.6, f32[3,8,16,128]{3,2,1,0:T(8,128)S(1)} %bitcast.44, ...), custom_call_target="tpu_custom_call" | custom-call | flops 1 | bytes 1 | tf_op jit(solution)/shard_map/local_step/pallas_call | solution.py:366
  15.7 0.7 collective-permute-start.3
  16.4 0.0 copy-start.5
  16.4 5.4 %collective-permute-start.4 = (f32[85,8,128]{2,1,0:T(8,128)S(1)}, f32[85,8,128]{2,1,0:T(8,128)S(1)}, u32[]{:S(2)}, u32[]{:S(2)}) collective-permute-start(f32[85,8,128]{2,1,0:T(8,128)S(1)} %get-tuple-element.19), channel_id=1, source_target_pairs={{0,1},{1,0},{2,3},{3,2},{4,5},{5,4},{6,7},{7,6},{8,9},{9,8},{10,11... | collective-permute-start | bytes 1044488 | tf_op jit(solution)/shard_map/ppermute | solution.py:338
  21.7 0.0 collective-permute-done.early
  21.7 0.0 collective-permute-done.3.late
  21.8 8.5 %collective-permute-done.4.r0 = f32[85,8,128]{2,1,0:T(8,128)S(1)} collective-permute-done((f32[85,8,128]{2,1,0:T(8,128)S(1)}, f32[85,8,128]{2,1,0:T(8,128)S(1)}, u32[]{:S(2)}, u32[]{:S(2)}) %collective-permute-start.4) | collective-permute-done | bytes 348192 | tf_op jit(solution)/shard_map/ppermute | solution.py:338
  30.3 0.0 copy-done.5
  30.3 1.9 %final_step.1 = (f32[3,8,16,128]{3,2,1,0:T(8,128)}, f32[3,8,16,128]{3,2,1,0:T(8,128)}, f32[1,128]{1,0:T(1,128)S(1)}) custom-call(f32[4]{0:T(128)S(1)} %copy-done.6, f32[3,8,16,128]{3,2,1,0:T(8,128)S(1)} %bitcast.45, f32[3,8,16,128]{3,2,1,0:T(8,128)S(1)} %bitcast.48, s32[8,16,128]{2,1,0:T(8,128)S(1)} %bitcast.55, s32[8,16,128]{2,1,0:T(8,128)S(1)} %bitcast.56, ...), custom_call_target="tpu_custom_call" | custom-call | tf_op jit(solution)/shard_map/final_step/pallas_call | solution.py:394
  32.2 24.5 %all_to_all.12 = f32[16,1,128]{2,1,0:T(1,128)S(1)} all-to-all(f32[16,1,128]{2,1,0:T(1,128)S(1)} %broadcast_in_dim.4), channel_id=1, replica_groups=mesh['zl'=4,'y'=8,'c'=2,'zh'=2,'x'=4] {'zl','zh','c'}, dimensions={0} | all-to-all | bytes 16384 | tf_op jit(solution)/shard_map/all_to_all | solution.py:344
  56.7 14.6 %all_to_all.13 = f32[32,1,128]{2,1,0:T(1,128)S(1)} all-to-all(f32[32,1,128]{2,1,0:T(1,128)S(1)} %broadcast_in_dim.5), channel_id=1, replica_groups=mesh['zl'=4,'y'=8,'c'=2,'zh'=2,'x'=4] {'y','x'}, dimensions={0} | all-to-all | bytes 32768 | tf_op jit(solution)/shard_map/all_to_all | solution.py:344
  71.3 0.5 slice_multiply_fusion
  (5 shorter events, 0.1 us)
Async XLA Ops:
  0.6 14.0 %copy-start = (f32[3,8,2,1024]{3,2,1,0:T(2,128)S(1)}, f32[3,8,2,1024]{3,2,1,0:T(2,128)}, u32[]{:S(2)}) copy-start(f32[3,8,2,1024]{3,2,1,0:T(2,128)} %param.7) | copy-start | bytes 589828
  0.6 14.0 %copy-start.1 = (f32[3,8,2,1024]{3,2,1,0:T(2,128)S(1)}, f32[3,8,2,1024]{3,2,1,0:T(2,128)}, u32[]{:S(2)}) copy-start(f32[3,8,2,1024]{3,2,1,0:T(2,128)} %param.9) | copy-start | bytes 589828
  0.7 14.0 %copy-start.2 = (f32[3,8,2,1024]{3,2,1,0:T(2,128)S(1)}, f32[3,8,2,1024]{3,2,1,0:T(2,128)}, u32[]{:S(2)}) copy-start(f32[3,8,2,1024]{3,2,1,0:T(2,128)} %param.8) | copy-start | bytes 589828
  0.7 14.0 %copy-start.3 = (f32[3,8,2,1024]{3,2,1,0:T(2,128)S(1)}, f32[3,8,2,1024]{3,2,1,0:T(2,128)}, u32[]{:S(2)}) copy-start(f32[3,8,2,1024]{3,2,1,0:T(2,128)} %param.10) | copy-start | bytes 589828
  0.7 14.0 %copy-start.4 = (s32[8,2,1024]{2,1,0:T(2,128)S(1)}, s32[8,2,1024]{2,1,0:T(2,128)}, u32[]{:S(2)}) copy-start(s32[8,2,1024]{2,1,0:T(2,128)} %param.11) | copy-start | bytes 196612
  3.2 18.5 %collective-permute-start = (f32[66,8,128]{2,1,0:T(8,128)}, f32[66,8,128]{2,1,0:T(8,128)S(1)}, u32[]{:S(2)}, u32[]{:S(2)}) collective-permute-start(f32[66,8,128]{2,1,0:T(8,128)} %get-tuple-element.15), channel_id=1, source_target_pairs={{1,2},{2,1},{3,4},{4,3},{5,6},{6,5},{9,10},{10,9},{11,12},{12,11},... | collective-permute-start | bytes 811016 | tf_op jit(solution)/shard_map/ppermute | solution.py:338
  3.9 10.8 %copy-start.6 = (f32[4]{0:T(128)S(1)}, f32[4]{0:T(128)}, u32[]{:S(2)}) copy-start(f32[4]{0:T(128)} %eps_ref.5) | copy-start | bytes 52
  3.9 9.5 %collective-permute-start.1 = (f32[26,16,128]{2,1,0:T(8,128)}, f32[26,16,128]{2,1,0:T(8,128)S(1)}, u32[]{:S(2)}, u32[]{:S(2)}) collective-permute-start(f32[26,16,128]{2,1,0:T(8,128)} %get-tuple-element.16), channel_id=1, source_target_pairs={{8,16},{16,8},{24,32},{32,24},{40,48},{48,40},{56,64},{64,56},{72,... | collective-permute-start | bytes 638984 | tf_op jit(solution)/shard_map/ppermute | solution.py:338
  8.5 6.2 %collective-permute-start.2 = (f32[26,16,128]{2,1,0:T(8,128)}, f32[26,16,128]{2,1,0:T(8,128)S(1)}, u32[]{:S(2)}, u32[]{:S(2)}) collective-permute-start(f32[26,16,128]{2,1,0:T(8,128)} %get-tuple-element.17), channel_id=1, source_target_pairs={{0,8},{8,0},{1,9},{9,1},{2,10},{10,2},{3,11},{11,3},{4,12},{12,4},... | collective-permute-start | bytes 638984 | tf_op jit(solution)/shard_map/ppermute | solution.py:338
  15.7 6.1 %collective-permute-start.3 = (f32[21,8,128]{2,1,0:T(8,128)S(1)}, f32[21,8,128]{2,1,0:T(8,128)S(1)}, u32[]{:S(2)}, u32[]{:S(2)}) collective-permute-start(f32[21,8,128]{2,1,0:T(8,128)S(1)} %get-tuple-element.18), channel_id=1, source_target_pairs={{1,2},{2,1},{3,4},{4,3},{5,6},{6,5},{9,10},{10,9},{11,12},{12,11},... | collective-permute-start | bytes 258056 | tf_op jit(solution)/shard_map/ppermute | solution.py:338
  16.4 13.9 %copy-start.5 = (s32[8,2,1024]{2,1,0:T(2,128)S(1)}, s32[8,2,1024]{2,1,0:T(2,128)}, u32[]{:S(2)}) copy-start(s32[8,2,1024]{2,1,0:T(2,128)} %param.12) | copy-start | bytes 196612
  16.4 13.9 %collective-permute-start.4 = (f32[85,8,128]{2,1,0:T(8,128)S(1)}, f32[85,8,128]{2,1,0:T(8,128)S(1)}, u32[]{:S(2)}, u32[]{:S(2)}) collective-permute-start(f32[85,8,128]{2,1,0:T(8,128)S(1)} %get-tuple-element.19), channel_id=1, source_target_pairs={{0,1},{1,0},{2,3},{3,2},{4,5},{5,4},{6,7},{7,6},{8,9},{9,8},{10,11... | collective-permute-start | bytes 1044488 | tf_op jit(solution)/shard_map/ppermute | solution.py:338

commit v5 on v3

--- a/solution.py
+++ b/solution.py
@@ -20,6 +20,7 @@
 DOWN = (("sx", 11, 2, 1), ("sy", 10, 1, 1), ("qx", 9, 1, 1), ("qy", 8, 1, 1))
 EARLY = 2 * 29 + 8
 LATE = 2 * 10 + 1
+AHEAD = 50
 HALO = 26
 
 
@@ -84,7 +85,7 @@
     values = coefs(eps)
 
     coef = [table(kinds[:, plane(z), :], values) for z in range(2)]
-    row = 0
+    ups, downs = [], []
     for chain in range(2):
         alpha, beta = ALPHA[chain], BETA[chain]
 
@@ -110,13 +111,14 @@
         s1z = sz[1][1:7] + b1[1:7] * ((ty[1][1:] - ty[1][:6]) - behind_y(tx[1][1:7]))
         px = tx[1][1:7] + alpha * (ahead_y(s1z) + s1y)
         py = ty[1][1:6] - alpha * (s1x[1:6] + (s1z[1:] - s1z[:5]))
-        up = jnp.concatenate([tx[1], ty[1], px, py, jnp.zeros((3, 8, 128), jnp.float32)], axis=0)
-        down = jnp.concatenate([sx[0], sy[0], qx, qy], axis=0)
-        early0[pl.ds(row, 29)] = jnp.where(even_z, up, down)
-        early1[pl.ds(row, 29)] = jnp.where(even_z, down, up)
-        row += 29
-    early0[pl.ds(row, 8)] = jnp.where(even_z, coef[1], coef[0])
-    early1[pl.ds(row, 8)] = jnp.where(even_z, coef[0], coef[1])
+        ups += [tx[1], ty[1], px, py, jnp.zeros((3, 8, 128), jnp.float32)]
+        downs += [sx[0], sy[0], qx, qy]
+        if chain == 0:
+            ups.append(coef[1])
+            downs.append(coef[0])
+    up, down = jnp.concatenate(ups, axis=0), jnp.concatenate(downs, axis=0)
+    early0[...] = jnp.where(even_z, up, down)[:AHEAD]
+    early1[...] = jnp.where(even_z, down, up)
 
     def put(line, first, last):
         pair_ref[line] = jnp.where(even, last, first)
@@ -135,6 +137,15 @@
     for value, (_, count, low, high) in zip(planes, layout):
         picked += [value[:low], value[count - high :]]
     return jnp.concatenate(picked, axis=0)
+
+
+def rest(planes, layout):
+    inner = [value[low : count - high] for value, (_, count, low, high) in zip(planes, layout)]
+    inner = jnp.concatenate(inner, axis=0)
+    missing = 29 - inner.shape[0]
+    if missing:
+        inner = jnp.concatenate([inner, jnp.zeros((missing, 8, 128), jnp.float32)], axis=0)
+    return inner[AHEAD - 37 :]
 
 
 def local_kernel(eps_ref, e, h, g, kf, m, next_ref, pair_ref, late0, late1, t1s, s1s, s0s, cs):
@@ -203,8 +214,13 @@
         late_down = jnp.concatenate([edges(down, DOWN), jnp.zeros((1, 8, 128), jnp.float32)], axis=0)
         late0[pl.ds(10 * chain, 10)] = jnp.where(even_z, late_up, late_down)
         late1[pl.ds(10 * chain, 10)] = jnp.where(even_z, late_down, late_up)
+    late0[pl.ds(LATE, EARLY - AHEAD)] = jnp.where(even_z, rest(up, UP), rest(down, DOWN))
     late0[20] = jnp.where(even_z, coef[1][10], coef[0][1])
     late1[20] = jnp.where(even_z, coef[0][1], coef[1][10])
+
+
+def take_kernel(*refs):
+    del refs
 
 
 def final_kernel(eps_ref, e, g, m, owner, early1, early0, late1, late0, t1s, s1s, s0s, cs, adj_e, adj_h, sums):
@@ -213,21 +229,35 @@
     values = coefs(eps_ref)
     inverse = [2.0 * eps_ref[kind] for kind in range(4)]
 
+    def early_even(start, count):
+        ahead = max(0, min(count, AHEAD - start))
+        parts = [early0[pl.ds(start, ahead)]] if ahead else []
+        if ahead < count:
+            parts.append(late0[pl.ds(LATE + start + ahead - AHEAD, count - ahead)])
+        return jnp.concatenate(parts, axis=0)
+
+    def early_up(start, count):
+        return jnp.where(even_z, early_even(start, count), early1[pl.ds(start, count)])
+
+    def early_low(start, count):
+        return jnp.where(even_z, early1[pl.ds(start, count)], early_even(start, count))
+
+    def late_up(start, count):
+        return jnp.where(even_z, late0[pl.ds(start, count)], late1[pl.ds(start, count)])
+
+    def late_low(start, count):
+        return jnp.where(even_z, late1[pl.ds(start, count)], late0[pl.ds(start, count)])
+
     def joined(early_lines, late_lines, layout, chain, at):
-        first, edge = 29 * chain, 10 * chain
+        first, edge = 37 * chain, 10 * chain
         for _, count, low, high in layout[:at]:
             first, edge = first + count - low - high, edge + low + high
         _, count, low, high = layout[at]
         middle = early_lines(first, count - low - high)
         return jnp.concatenate([late_lines(edge, low), middle, late_lines(edge + low, high)], axis=0)
 
-    def select(if_even, if_odd):
-        return lambda start, count: jnp.where(even_z, if_even[pl.ds(start, count)], if_odd[pl.ds(start, count)])
-
-    early_up, late_up = select(early0, early1), select(late0, late1)
-    early_low, late_low = select(early1, early0), select(late1, late0)
-    c_up = jnp.concatenate([late_up(20, 1), early_up(58, 8)], axis=0)
-    c_low = jnp.concatenate([early_low(58, 8), late_low(20, 1)], axis=0)
+    c_up = jnp.concatenate([late_up(20, 1), early_up(29, 8)], axis=0)
+    c_low = jnp.concatenate([early_low(29, 8), late_low(20, 1)], axis=0)
     own = slice(1, 9)
     kept = []
     for chain in range(2):
@@ -298,7 +328,9 @@
 
 VMEM = pl.BlockSpec(memory_space=pltpu.VMEM)
 SMEM = pl.BlockSpec(memory_space=pltpu.SMEM)
+ANY = pl.BlockSpec(memory_space=pl.ANY)
 HBM = pl.BlockSpec(memory_space=pltpu.HBM)
+TAKE = 2 * 10**10
 LARGE = 62 * 1024 * 1024
 PARAMS = pltpu.CompilerParams(vmem_limit_bytes=48 * 1024 * 1024)
 
@@ -337,7 +369,7 @@
     e, h, g, k, m, own = (rows(u) for u in (e_check, h_check, adj_e, adj_h, material, owner))
     pair, following, early0, early1 = pl.pallas_call(
         pack_kernel,
-        out_shape=(f32(HALO, 16, 128), f32(HALO, 16, 128), f32(EARLY, 8, 128), f32(EARLY, 8, 128)),
+        out_shape=(f32(HALO, 16, 128), f32(HALO, 16, 128), f32(AHEAD, 8, 128), f32(EARLY, 8, 128)),
         in_specs=[HBM] * 6,
         out_specs=[VMEM] * 4,
         scratch_shapes=[
@@ -356,7 +388,7 @@
     late0, late1, t1s, s1s, s0s, cs = pl.pallas_call(
         local_kernel,
         out_shape=(
-            f32(LATE, 8, 128),
+            f32(LATE + EARLY - AHEAD, 8, 128),
             f32(LATE, 8, 128),
             f32(2, 3, 2, 11, 8, 128),
             f32(2, 3, 2, 10, 8, 128),
@@ -369,8 +401,18 @@
         cost_estimate=pl.CostEstimate(flops=1, bytes_accessed=1, transcendentals=0),
         name="local_step",
     )(permittivity, e, h, g, k, m, following, pair)
+    late0 = swap_pairs(late0, "x", 0)
     late1 = swap_pairs(late1, GZ, 1)
-    late0 = swap_pairs(late0, "x", 0)
+    early1, early0 = pl.pallas_call(
+        take_kernel,
+        out_shape=(f32(EARLY, 8, 128), f32(AHEAD, 8, 128)),
+        in_specs=[ANY] * 2,
+        out_specs=[ANY] * 2,
+        input_output_aliases={0: 0, 1: 1},
+        compiler_params=PARAMS,
+        cost_estimate=pl.CostEstimate(flops=TAKE, bytes_accessed=10**9, transcendentals=0),
+        name="take_early",
+    )(early1, early0)
     out_e, out_h, sums = pl.pallas_call(
         final_kernel,
         out_shape=(f32(3, 8, 16, 128), f32(3, 8, 16, 128), f32(1, 128)),

time: 71 us -> 69.6 us (0.980)
  blocking collectives: 35.6 us -> 32.7 us
  waiting for transfers between devices: 1.84 us -> 3.18 us
    all_to_all x2, blocking collectives: 35.6 us -> 32.7 us  [spread_sum(): return jnp.sum(lax.all_to_all(sent, axes, 0, 0), axis=0)]
    ppermute x6, waiting for transfers between devices: 1.84 us -> 3.18 us  [swap_pairs(): return lax.ppermute(value, axes, pairs)]
where the time goes in v5:
time: 69.6 us; the launch traced here: 69.2 us
  blocking collectives  32.7 us (47%)
  starting transfers between devices  26.5 us (38%)
  Pallas kernels  5.43 us (8%)
  waiting for transfers between devices  3.18 us (5%)
  between operations  0.84 us (1%)
    all_to_all x2, blocking collectives, spread_sum(): return jnp.sum(lax.all_to_all(sent, axes, 0, 0), axis=0)  32.7 us
    ppermute x6, starting transfers between devices, swap_pairs(): return lax.ppermute(value, axes, pairs)  26.5 us
    ppermute x6, waiting for transfers between devices, swap_pairs(): return lax.ppermute(value, axes, pairs)  3.18 us
    pallas_call x1, Pallas kernels, body(): pl.pallas_call(pack_kernel, out_shape=(f32(HALO, 16, 128), f32(HALO, 16,...  2.6 us
    pallas_call x1, Pallas kernels, body(): pl.pallas_call(final_kernel, out_shape=(f32(3, 8, 16, 128), f32(3, 8, 16,...  1.87 us
  transfers between devices with their start and end apart: 6, of which 1 were waited for; matrix products, arithmetic and copies ran while one was open for 0% of the time, Pallas kernels for 1%

profile of v5, /device:TPU:1, one launch (start us, length us, event | category | flops | bytes accessed | tf_op | source)
XLA Modules:
  0.0 69.2 jit_solution(3862082006301541061)
XLA Ops:
  0.6 0.0 copy-start
  0.6 0.0 copy-start.1
  0.7 0.0 copy-start.2
  0.7 0.0 copy-start.3
  0.7 0.0 copy-start.4
  0.7 2.6 %pack.1 = (f32[26,16,128]{2,1,0:T(8,128)}, f32[26,16,128]{2,1,0:T(8,128)}, f32[50,8,128]{2,1,0:T(8,128)}, f32[66,8,128]{2,1,0:T(8,128)}) custom-call(f32[4]{0:T(128)} %eps_ref.5, f32[3,8,16,128]{3,2,1,0:T(8,128)} %bitcast.43, f32[3,8,16,128]{3,2,1,0:T(8,128)} %bitcast.49, f32[3,8,16,128]{3,2,1,0:T(8,128)} %bitcast.46, f32[3,8,16,128]{3,2,1,0:T(8,128)} %bitcast.51, ...), custom_call_target="tpu_custom_call" | custom-call | tf_op jit(solution)/shard_map/pack/pallas_call | solution.py:370
  3.3 0.7 collective-permute-start
  4.0 4.6 %collective-permute-start.2 = (f32[26,16,128]{2,1,0:T(8,128)}, f32[26,16,128]{2,1,0:T(8,128)S(1)}, u32[]{:S(2)}, u32[]{:S(2)}) collective-permute-start(f32[26,16,128]{2,1,0:T(8,128)} %get-tuple-element.22), channel_id=1, source_target_pairs={{8,16},{16,8},{24,32},{32,24},{40,48},{48,40},{56,64},{64,56},{72,... | collective-permute-start | bytes 638984 | tf_op jit(solution)/shard_map/ppermute | solution.py:359
  8.6 0.0 copy-start.6
  8.6 4.9 %collective-permute-start.3 = (f32[26,16,128]{2,1,0:T(8,128)}, f32[26,16,128]{2,1,0:T(8,128)S(1)}, u32[]{:S(2)}, u32[]{:S(2)}) collective-permute-start(f32[26,16,128]{2,1,0:T(8,128)} %get-tuple-element.23), channel_id=1, source_target_pairs={{0,8},{8,0},{1,9},{9,1},{2,10},{10,2},{3,11},{11,3},{4,12},{12,4},... | collective-permute-start | bytes 638984 | tf_op jit(solution)/shard_map/ppermute | solution.py:359
  13.5 2.9 %collective-permute-start.1 = (f32[50,8,128]{2,1,0:T(8,128)}, f32[50,8,128]{2,1,0:T(8,128)S(1)}, u32[]{:S(2)}, u32[]{:S(2)}) collective-permute-start(f32[50,8,128]{2,1,0:T(8,128)} %get-tuple-element.19), channel_id=1, source_target_pairs={{0,1},{1,0},{2,3},{3,2},{4,5},{5,4},{6,7},{7,6},{8,9},{9,8},{10,11... | collective-permute-start | bytes 614408 | tf_op jit(solution)/shard_map/ppermute | solution.py:359
  16.4 0.0 collective-permute-done.2.next_ref
  16.4 0.0 collective-permute-done.3.pair_ref
  16.4 0.0 copy-done
  16.4 0.0 copy-done.1
  16.4 0.0 copy-done.2
  16.4 0.0 copy-done.3
  16.4 0.0 copy-done.4
  16.4 0.0 copy-done.6
  16.4 1.0 %local_step.1 = (f32[37,8,128]{2,1,0:T(8,128)S(1)}, f32[21,8,128]{2,1,0:T(8,128)S(1)}, f32[2,3,2,11,8,128]{5,4,3,2,1,0:T(8,128)S(1)}, f32[2,3,2,10,8,128]{5,4,3,...) custom-call(f32[4]{0:T(128)S(1)} %copy-done.6, f32[3,8,16,128]{3,2,1,0:T(8,128)S(1)} %bitcast.44, ...), custom_call_target="tpu_custom_call" | custom-call | flops 1 | bytes 1 | tf_op jit(solution)/shard_map/local_step/pallas_call | solution.py:388
  17.4 0.7 collective-permute-start.4
  18.1 0.0 copy-start.5
  18.1 12.8 %collective-permute-start.5 = (f32[37,8,128]{2,1,0:T(8,128)S(1)}, f32[37,8,128]{2,1,0:T(8,128)S(1)}, u32[]{:S(2)}, u32[]{:S(2)}) collective-permute-start(f32[37,8,128]{2,1,0:T(8,128)S(1)} %get-tuple-element.25), channel_id=1, source_target_pairs={{0,1},{1,0},{2,3},{3,2},{4,5},{5,4},{6,7},{7,6},{8,9},{9,8},{10,11... | collective-permute-start | bytes 454664 | tf_op jit(solution)/shard_map/ppermute | solution.py:359
  30.9 0.0 collective-permute-done.1.refs_1_
  31.0 0.0 collective-permute-done.refs_0_
  31.0 0.0 collective-permute-done.4.late1
  31.0 3.2 %collective-permute-done.5.late0 = f32[37,8,128]{2,1,0:T(8,128)S(1)} collective-permute-done((f32[37,8,128]{2,1,0:T(8,128)S(1)}, f32[37,8,128]{2,1,0:T(8,128)S(1)}, u32[]{:S(2)}, u32[]{:S(2)}) %collective-permute-start.5) | collective-permute-done | bytes 151584 | tf_op jit(solution)/shard_map/ppermute | solution.py:359
  34.2 0.0 copy-done.5
  34.2 1.9 %final_step.1 = (f32[3,8,16,128]{3,2,1,0:T(8,128)}, f32[3,8,16,128]{3,2,1,0:T(8,128)}, f32[1,128]{1,0:T(1,128)S(1)}) custom-call(f32[4]{0:T(128)S(1)} %copy-done.6, f32[3,8,16,128]{3,2,1,0:T(8,128)S(1)} %bitcast.45, f32[3,8,16,128]{3,2,1,0:T(8,128)S(1)} %bitcast.48, s32[8,16,128]{2,1,0:T(8,128)S(1)} %bitcast.55, s32[8,16,128]{2,1,0:T(8,128)S(1)} %bitcast.56, ...), custom_call_target="tpu_custom_call" | custom-call | tf_op jit(solution)/shard_map/final_step/pallas_call | solution.py:416
  36.0 17.4 %all_to_all.12 = f32[16,1,128]{2,1,0:T(1,128)S(1)} all-to-all(f32[16,1,128]{2,1,0:T(1,128)S(1)} %broadcast_in_dim.4), channel_id=1, replica_groups=mesh['zl'=4,'y'=8,'c'=2,'zh'=2,'x'=4] {'zl','zh','c'}, dimensions={0} | all-to-all | bytes 16384 | tf_op jit(solution)/shard_map/all_to_all | solution.py:365
  53.4 15.3 %all_to_all.13 = f32[32,1,128]{2,1,0:T(1,128)S(1)} all-to-all(f32[32,1,128]{2,1,0:T(1,128)S(1)} %broadcast_in_dim.5), channel_id=1, replica_groups=mesh['zl'=4,'y'=8,'c'=2,'zh'=2,'x'=4] {'y','x'}, dimensions={0} | all-to-all | bytes 32768 | tf_op jit(solution)/shard_map/all_to_all | solution.py:365
  68.7 0.5 slice_multiply_fusion
  (5 shorter events, 0.1 us)
Async XLA Ops:
  0.6 15.8 %copy-start = (f32[3,8,2,1024]{3,2,1,0:T(2,128)S(1)}, f32[3,8,2,1024]{3,2,1,0:T(2,128)}, u32[]{:S(2)}) copy-start(f32[3,8,2,1024]{3,2,1,0:T(2,128)} %param.7) | copy-start | bytes 589828
  0.6 15.8 %copy-start.1 = (f32[3,8,2,1024]{3,2,1,0:T(2,128)S(1)}, f32[3,8,2,1024]{3,2,1,0:T(2,128)}, u32[]{:S(2)}) copy-start(f32[3,8,2,1024]{3,2,1,0:T(2,128)} %param.9) | copy-start | bytes 589828
  0.7 15.8 %copy-start.2 = (f32[3,8,2,1024]{3,2,1,0:T(2,128)S(1)}, f32[3,8,2,1024]{3,2,1,0:T(2,128)}, u32[]{:S(2)}) copy-start(f32[3,8,2,1024]{3,2,1,0:T(2,128)} %param.8) | copy-start | bytes 589828
  0.7 15.8 %copy-start.3 = (f32[3,8,2,1024]{3,2,1,0:T(2,128)S(1)}, f32[3,8,2,1024]{3,2,1,0:T(2,128)}, u32[]{:S(2)}) copy-start(f32[3,8,2,1024]{3,2,1,0:T(2,128)} %param.10) | copy-start | bytes 589828
  0.7 15.8 %copy-start.4 = (s32[8,2,1024]{2,1,0:T(2,128)S(1)}, s32[8,2,1024]{2,1,0:T(2,128)}, u32[]{:S(2)}) copy-start(s32[8,2,1024]{2,1,0:T(2,128)} %param.11) | copy-start | bytes 196612
  3.3 27.7 %collective-permute-start = (f32[66,8,128]{2,1,0:T(8,128)}, f32[66,8,128]{2,1,0:T(8,128)S(1)}, u32[]{:S(2)}, u32[]{:S(2)}) collective-permute-start(f32[66,8,128]{2,1,0:T(8,128)} %get-tuple-element.18), channel_id=1, source_target_pairs={{1,2},{2,1},{3,4},{4,3},{5,6},{6,5},{9,10},{10,9},{11,12},{12,11},... | collective-permute-start | bytes 811016 | tf_op jit(solution)/shard_map/ppermute | solution.py:359
  4.0 12.4 %collective-permute-start.2 = (f32[26,16,128]{2,1,0:T(8,128)}, f32[26,16,128]{2,1,0:T(8,128)S(1)}, u32[]{:S(2)}, u32[]{:S(2)}) collective-permute-start(f32[26,16,128]{2,1,0:T(8,128)} %get-tuple-element.22), channel_id=1, source_target_pairs={{8,16},{16,8},{24,32},{32,24},{40,48},{48,40},{56,64},{64,56},{72,... | collective-permute-start | bytes 638984 | tf_op jit(solution)/shard_map/ppermute | solution.py:359
  8.6 7.9 %copy-start.6 = (f32[4]{0:T(128)S(1)}, f32[4]{0:T(128)}, u32[]{:S(2)}) copy-start(f32[4]{0:T(128)} %eps_ref.5) | copy-start | bytes 52
  8.6 7.8 %collective-permute-start.3 = (f32[26,16,128]{2,1,0:T(8,128)}, f32[26,16,128]{2,1,0:T(8,128)S(1)}, u32[]{:S(2)}, u32[]{:S(2)}) collective-permute-start(f32[26,16,128]{2,1,0:T(8,128)} %get-tuple-element.23), channel_id=1, source_target_pairs={{0,8},{8,0},{1,9},{9,1},{2,10},{10,2},{3,11},{11,3},{4,12},{12,4},... | collective-permute-start | bytes 638984 | tf_op jit(solution)/shard_map/ppermute | solution.py:359
  13.5 17.5 %collective-permute-start.1 = (f32[50,8,128]{2,1,0:T(8,128)}, f32[50,8,128]{2,1,0:T(8,128)S(1)}, u32[]{:S(2)}, u32[]{:S(2)}) collective-permute-start(f32[50,8,128]{2,1,0:T(8,128)} %get-tuple-element.19), channel_id=1, source_target_pairs={{0,1},{1,0},{2,3},{3,2},{4,5},{5,4},{6,7},{7,6},{8,9},{9,8},{10,11... | collective-permute-start | bytes 614408 | tf_op jit(solution)/shard_map/ppermute | solution.py:359
  17.4 13.6 %collective-permute-start.4 = (f32[21,8,128]{2,1,0:T(8,128)S(1)}, f32[21,8,128]{2,1,0:T(8,128)S(1)}, u32[]{:S(2)}, u32[]{:S(2)}) collective-permute-start(f32[21,8,128]{2,1,0:T(8,128)S(1)} %get-tuple-element.24), channel_id=1, source_target_pairs={{1,2},{2,1},{3,4},{4,3},{5,6},{6,5},{9,10},{10,9},{11,12},{12,11},... | collective-permute-start | bytes 258056 | tf_op jit(solution)/shard_map/ppermute | solution.py:359
  18.1 16.1 %copy-start.5 = (s32[8,2,1024]{2,1,0:T(2,128)S(1)}, s32[8,2,1024]{2,1,0:T(2,128)}, u32[]{:S(2)}) copy-start(s32[8,2,1024]{2,1,0:T(2,128)} %param.12) | copy-start | bytes 196612
  18.1 16.1 %collective-permute-start.5 = (f32[37,8,128]{2,1,0:T(8,128)S(1)}, f32[37,8,128]{2,1,0:T(8,128)S(1)}, u32[]{:S(2)}, u32[]{:S(2)}) collective-permute-start(f32[37,8,128]{2,1,0:T(8,128)S(1)} %get-tuple-element.25), channel_id=1, source_target_pairs={{0,1},{1,0},{2,3},{3,2},{4,5},{5,4},{6,7},{7,6},{8,9},{9,8},{10,11... | collective-permute-start | bytes 454664 | tf_op jit(solution)/shard_map/ppermute | solution.py:359

commit v6 on v5

--- a/solution.py
+++ b/solution.py
@@ -20,8 +20,8 @@
 DOWN = (("sx", 11, 2, 1), ("sy", 10, 1, 1), ("qx", 9, 1, 1), ("qy", 8, 1, 1))
 EARLY = 2 * 29 + 8
 LATE = 2 * 10 + 1
-AHEAD = 50
-HALO = 26
+AHEAD = 40
+HALO = 13
 
 
 def shift_later(u):
@@ -72,17 +72,31 @@
     return jnp.where(first, 0.0, 1.0).astype(jnp.float32)
 
 
-def pack_kernel(eps_ref, e, h, g, k, m, pair_ref, next_ref, early0, early1, eps, fields, kinds, sems):
-    copies = [pltpu.make_async_copy(eps_ref, eps, sems.at[5]), pltpu.make_async_copy(m, kinds, sems.at[4])]
-    for field, ref in enumerate((e, h, g, k)):
-        copies.append(pltpu.make_async_copy(ref, fields.at[field], sems.at[field]))
-    for copy in copies:
+def pack_kernel(eps_ref, e, h, g, k, m, pair_ref, next_ref, early0, early1, eps, fields, kinds, edge, lines0, lines1, sems, outs):
+    kinds_in = pltpu.make_async_copy(m, kinds, sems.at[4])
+    eps_in = pltpu.make_async_copy(eps_ref, eps, sems.at[5])
+    fields_in = [pltpu.make_async_copy(ref, fields.at[i], sems.at[i]) for i, ref in enumerate((e, h, g, k))]
+    for copy in (kinds_in, eps_in, *fields_in):
         copy.start()
-    for copy in copies:
-        copy.wait()
     even = lax.axis_index("c") == 0
     even_z = lax.axis_index("x") % 2 == 0
+    sides = ((jnp.where(even, 6, 0), pair_ref), (jnp.where(even, 0, 6), next_ref))
+    sent = []
+
+    def send(source, target, at):
+        sent.append(pltpu.make_async_copy(source, target, outs.at[at]))
+        sent[-1].start()
+
+    kinds_in.wait()
+    eps_in.wait()
     values = coefs(eps)
+    for side, (start, out) in enumerate(sides):
+        edge[side] = table(kinds[pl.ds(start, 2)], values)
+        send(edge.at[side], out.at[12], side * 5 + 4)
+    for field, copy in enumerate(fields_in):
+        copy.wait()
+        for side, (start, out) in enumerate(sides):
+            send(fields.at[field, :, pl.ds(start, 2)], out.at[3 * field : 3 * field + 3], side * 5 + field)
 
     coef = [table(kinds[:, plane(z), :], values) for z in range(2)]
     ups, downs = [], []
@@ -117,19 +131,12 @@
             ups.append(coef[1])
             downs.append(coef[0])
     up, down = jnp.concatenate(ups, axis=0), jnp.concatenate(downs, axis=0)
-    early0[...] = jnp.where(even_z, up, down)[:AHEAD]
-    early1[...] = jnp.where(even_z, down, up)
-
-    def put(line, first, last):
-        pair_ref[line] = jnp.where(even, last, first)
-        next_ref[line] = jnp.where(even, first, last)
-
-    for field in range(4):
-        for comp in range(3):
-            for line in range(2):
-                put(field * 6 + comp * 2 + line, fields[field, comp, line], fields[field, comp, 6 + line])
-    for line in range(2):
-        put(24 + line, table(kinds[line], values), table(kinds[6 + line], values))
+    lines1[...] = jnp.where(even_z, down, up)
+    send(lines1, early1, 10)
+    lines0[...] = jnp.where(even_z, up, down)[:AHEAD]
+    send(lines0, early0, 11)
+    for copy in sent:
+        copy.wait()
 
 
 def edges(planes, layout):
@@ -155,10 +162,10 @@
     values = coefs(eps_ref)
 
     def below(row, z):
-        return jnp.where(even_x, next_ref[row, plane(z), :], pair_ref[row, plane(z), :])[None]
+        return jnp.where(even_x, next_ref[row // 2, row % 2, plane(z), :], pair_ref[row // 2, row % 2, plane(z), :])[None]
 
     def above(row, z):
-        return jnp.where(even_x, pair_ref[row, plane(z), :], next_ref[row, plane(z), :])[None]
+        return jnp.where(even_x, pair_ref[row // 2, row % 2, plane(z), :], next_ref[row // 2, row % 2, plane(z), :])[None]
 
     def extended(ref, base, comp, z):
         row = base + comp * 2
@@ -223,7 +230,7 @@
     del refs
 
 
-def final_kernel(eps_ref, e, g, m, owner, early1, early0, late1, late0, t1s, s1s, s0s, cs, adj_e, adj_h, sums):
+def final_kernel(eps_ref, e, g, m, owner, early1, early0, late1, late0, t1s, s1s, s0s, cs, adj_e, adj_h, sums, new_e, new_h, outs):
     even_z = lax.axis_index("x") % 2 == 0
     x_flag, z_flag = low_flag(XY), low_flag(GZ)
     values = coefs(eps_ref)
@@ -259,8 +266,9 @@
     c_up = jnp.concatenate([late_up(20, 1), early_up(29, 8)], axis=0)
     c_low = jnp.concatenate([early_low(29, 8), late_low(20, 1)], axis=0)
     own = slice(1, 9)
-    kept = []
-    for chain in range(2):
+    kept = [None, None]
+    writes = [pltpu.make_async_copy(new_e, adj_e, outs.at[0]), pltpu.make_async_copy(new_h, adj_h, outs.at[1])]
+    for chain in (1, 0):
         alpha, beta = ALPHA[chain], BETA[chain]
         sx2, sy2, qx, qy = (joined(early_up, late_up, DOWN, chain, at) for at in range(4))
         ax, ay, px, py = (joined(early_low, late_low, UP, chain, at) for at in range(4))
@@ -300,13 +308,15 @@
                 dz_x - (t2z[z][1:] - t2z[z][:8]),
                 (t2y[z][1:] - t2y[z][:8]) - behind_y(t2x[z]),
             ))
-        kept.append(([[s[z][own] for s in (sx, sy, sz)] for z in range(2)], curl))
+        kept[chain] = ([[s[z][own] for s in (sx, sy, sz)] for z in range(2)], curl)
         if chain == 1:
             for z in range(2):
                 scale = table(m[:, plane(z), :], inverse)
                 for comp, t2 in enumerate((t2x[z], t2y[z][1:], t2z[z][1:])):
-                    adj_e[comp, :, plane(z), :] = kept[1][0][z][comp] * scale - COURANT * curl[z][comp]
-                    adj_h[comp, :, plane(z), :] = t2
+                    new_e[comp, :, plane(z), :] = kept[1][0][z][comp] * scale - COURANT * curl[z][comp]
+                    new_h[comp, :, plane(z), :] = t2
+            for copy in writes:
+                copy.start()
 
     totals = [jnp.zeros((8, 128), jnp.float32) for _ in range(NI)]
     for z in range(2):
@@ -324,6 +334,8 @@
     for j in range(NI):
         row = row + jnp.where(lane == j, jnp.sum(totals[j]), 0.0)
     sums[...] = jnp.broadcast_to(row, sums.shape)
+    for copy in writes:
+        copy.wait()
 
 
 VMEM = pl.BlockSpec(memory_space=pltpu.VMEM)
@@ -369,14 +381,18 @@
     e, h, g, k, m, own = (rows(u) for u in (e_check, h_check, adj_e, adj_h, material, owner))
     pair, following, early0, early1 = pl.pallas_call(
         pack_kernel,
-        out_shape=(f32(HALO, 16, 128), f32(HALO, 16, 128), f32(AHEAD, 8, 128), f32(EARLY, 8, 128)),
+        out_shape=(f32(HALO, 2, 16, 128), f32(HALO, 2, 16, 128), f32(AHEAD, 8, 128), f32(EARLY, 8, 128)),
         in_specs=[HBM] * 6,
-        out_specs=[VMEM] * 4,
+        out_specs=[HBM] * 4,
         scratch_shapes=[
             pltpu.SMEM((4,), jnp.float32),
             pltpu.VMEM((4, 3, 8, 16, 128), jnp.float32),
             pltpu.VMEM((8, 16, 128), jnp.int32),
+            pltpu.VMEM((2, 2, 16, 128), jnp.float32),
+            pltpu.VMEM((AHEAD, 8, 128), jnp.float32),
+            pltpu.VMEM((EARLY, 8, 128), jnp.float32),
             pltpu.SemaphoreType.DMA((6,)),
+            pltpu.SemaphoreType.DMA((12,)),
         ],
         compiler_params=pltpu.CompilerParams(vmem_limit_bytes=LARGE),
         name="pack",
@@ -417,7 +433,12 @@
         final_kernel,
         out_shape=(f32(3, 8, 16, 128), f32(3, 8, 16, 128), f32(1, 128)),
         in_specs=[SMEM] + [VMEM] * 12,
-        out_specs=[VMEM] * 3,
+        out_specs=[HBM, HBM, VMEM],
+        scratch_shapes=[
+            pltpu.VMEM((3, 8, 16, 128), jnp.float32),
+            pltpu.VMEM((3, 8, 16, 128), jnp.float32),
+            pltpu.SemaphoreType.DMA((2,)),
+        ],
         compiler_params=PARAMS,
         name="final_step",
     )(permittivity, e, g, m, own, early1, early0, late1, late0, t1s, s1s, s0s, cs)

time: 69.6 us -> 69.6 us (level)
  blocking collectives: 32.7 us -> 31.8 us
  waiting for transfers between devices: 3.18 us -> 4.06 us
    ppermute x6, waiting for transfers between devices: 3.18 us -> 4.06 us  [swap_pairs(): return lax.ppermute(value, axes, pairs)]
    all_to_all x2, blocking collectives: 32.7 us -> 31.8 us  [spread_sum(): return jnp.sum(lax.all_to_all(sent, axes, 0, 0), axis=0)]
where the time goes in v6:
time: 69.6 us; the launch traced here: 69.2 us
  blocking collectives  31.8 us (46%)
  starting transfers between devices  26.5 us (38%)
  Pallas kernels  5.34 us (8%)
  waiting for transfers between devices  4.06 us (6%)
  between operations  0.86 us (1%)
    all_to_all x2, blocking collectives, spread_sum(): return jnp.sum(lax.all_to_all(sent, axes, 0, 0), axis=0)  31.8 us
    ppermute x6, starting transfers between devices, swap_pairs(): return lax.ppermute(value, axes, pairs)  26.5 us
    ppermute x6, waiting for transfers between devices, swap_pairs(): return lax.ppermute(value, axes, pairs)  4.06 us
    pallas_call x1, Pallas kernels, body(): pl.pallas_call(pack_kernel, out_shape=(f32(HALO, 2, 16, 128), f32(HALO, 2...  2.48 us
    pallas_call x1, Pallas kernels, body(): pl.pallas_call(final_kernel, out_shape=(f32(3, 8, 16, 128), f32(3, 8, 16,...  1.9 us
  transfers between devices with their start and end apart: 6, of which 1 were waited for; matrix products, arithmetic and copies ran while one was open for 0% of the time, Pallas kernels for 1%

profile of v6, /device:TPU:1, one launch (start us, length us, event | category | flops | bytes accessed | tf_op | source)
XLA Modules:
  0.0 69.2 jit_solution(6969271149688167058)
XLA Ops:
  0.6 0.0 copy-start
  0.6 0.0 copy-start.1
  0.7 0.0 copy-start.2
  0.7 0.0 copy-start.3
  0.7 0.0 copy-start.4
  0.7 2.5 %pack.1 = (f32[13,2,16,128]{3,2,1,0:T(8,128)}, f32[13,2,16,128]{3,2,1,0:T(8,128)}, f32[40,8,128]{2,1,0:T(8,128)}, f32[66,8,128]{2,1,0:T(8,128)}) custom-call(f32[4]{0:T(128)} %eps_ref.5, f32[3,8,16,128]{3,2,1,0:T(8,128)} %bitcast.43, f32[3,8,16,128]{3,2,1,0:T(8,128)} %bitcast.49, f32[3,8,16,128]{3,2,1,0:T(8,128)} %bitcast.46, f32[3,8,16,128]{3,2,1,0:T(8,128)} %bitcast.51, ...), custom_call_target="tpu_custom_call" | custom-call | tf_op jit(solution)/shard_map/pack/pallas_call | solution.py:382
  3.2 0.7 collective-permute-start
  3.9 4.6 %collective-permute-start.2 = (f32[13,2,16,128]{3,2,1,0:T(8,128)}, f32[13,2,16,128]{3,2,1,0:T(8,128)S(1)}, u32[]{:S(2)}, u32[]{:S(2)}) collective-permute-start(f32[13,2,16,128]{3,2,1,0:T(8,128)} %get-tuple-element.22), channel_id=1, source_target_pairs={{8,16},{16,8},{24,32},{32,24},{40,48},{48,40},{56,64},{64,56},{72,... | collective-permute-start | bytes 638984 | tf_op jit(solution)/shard_map/ppermute | solution.py:371
  8.5 0.0 copy-start.6
  8.5 4.9 %collective-permute-start.3 = (f32[13,2,16,128]{3,2,1,0:T(8,128)}, f32[13,2,16,128]{3,2,1,0:T(8,128)S(1)}, u32[]{:S(2)}, u32[]{:S(2)}) collective-permute-start(f32[13,2,16,128]{3,2,1,0:T(8,128)} %get-tuple-element.23), channel_id=1, source_target_pairs={{0,8},{8,0},{1,9},{9,1},{2,10},{10,2},{3,11},{11,3},{4,12},{12,4},... | collective-permute-start | bytes 638984 | tf_op jit(solution)/shard_map/ppermute | solution.py:371
  13.3 2.9 %collective-permute-start.1 = (f32[40,8,128]{2,1,0:T(8,128)}, f32[40,8,128]{2,1,0:T(8,128)S(1)}, u32[]{:S(2)}, u32[]{:S(2)}) collective-permute-start(f32[40,8,128]{2,1,0:T(8,128)} %get-tuple-element.19), channel_id=1, source_target_pairs={{0,1},{1,0},{2,3},{3,2},{4,5},{5,4},{6,7},{7,6},{8,9},{9,8},{10,11... | collective-permute-start | bytes 491528 | tf_op jit(solution)/shard_map/ppermute | solution.py:371
  16.2 0.0 collective-permute-done.2.next_ref
  16.3 0.0 collective-permute-done.3.pair_ref
  16.3 0.0 copy-done
  16.3 0.0 copy-done.1
  16.3 0.0 copy-done.2
  16.3 0.0 copy-done.3
  16.3 0.0 copy-done.4
  16.3 0.0 copy-done.6
  16.3 1.0 %local_step.1 = (f32[47,8,128]{2,1,0:T(8,128)S(1)}, f32[21,8,128]{2,1,0:T(8,128)S(1)}, f32[2,3,2,11,8,128]{5,4,3,2,1,0:T(8,128)S(1)}, f32[2,3,2,10,8,128]{5,4,3,...) custom-call(f32[4]{0:T(128)S(1)} %copy-done.6, f32[3,8,16,128]{3,2,1,0:T(8,128)S(1)} %bitcast.44, ...), custom_call_target="tpu_custom_call" | custom-call | flops 1 | bytes 1 | tf_op jit(solution)/shard_map/local_step/pallas_call | solution.py:404
  17.3 0.7 collective-permute-start.4
  18.0 0.0 copy-start.5
  18.0 12.8 %collective-permute-start.5 = (f32[47,8,128]{2,1,0:T(8,128)S(1)}, f32[47,8,128]{2,1,0:T(8,128)S(1)}, u32[]{:S(2)}, u32[]{:S(2)}) collective-permute-start(f32[47,8,128]{2,1,0:T(8,128)S(1)} %get-tuple-element.25), channel_id=1, source_target_pairs={{0,1},{1,0},{2,3},{3,2},{4,5},{5,4},{6,7},{7,6},{8,9},{9,8},{10,11... | collective-permute-start | bytes 577544 | tf_op jit(solution)/shard_map/ppermute | solution.py:371
  30.8 0.0 collective-permute-done.1.refs_1_
  30.8 0.0 collective-permute-done.refs_0_
  30.9 0.0 collective-permute-done.4.late1
  30.9 4.0 %collective-permute-done.5.late0 = f32[47,8,128]{2,1,0:T(8,128)S(1)} collective-permute-done((f32[47,8,128]{2,1,0:T(8,128)S(1)}, f32[47,8,128]{2,1,0:T(8,128)S(1)}, u32[]{:S(2)}, u32[]{:S(2)}) %collective-permute-start.5) | collective-permute-done | bytes 192544 | tf_op jit(solution)/shard_map/ppermute | solution.py:371
  34.9 0.0 copy-done.5
  34.9 1.9 %final_step.1 = (f32[3,8,16,128]{3,2,1,0:T(8,128)}, f32[3,8,16,128]{3,2,1,0:T(8,128)}, f32[1,128]{1,0:T(1,128)S(1)}) custom-call(f32[4]{0:T(128)S(1)} %copy-done.6, f32[3,8,16,128]{3,2,1,0:T(8,128)S(1)} %bitcast.45, f32[3,8,16,128]{3,2,1,0:T(8,128)S(1)} %bitcast.48, s32[8,16,128]{2,1,0:T(8,128)S(1)} %bitcast.55, s32[8,16,128]{2,1,0:T(8,128)S(1)} %bitcast.56, ...), custom_call_target="tpu_custom_call" | custom-call | tf_op jit(solution)/shard_map/final_step/pallas_call | solution.py:432
  36.8 17.2 %all_to_all.12 = f32[16,1,128]{2,1,0:T(1,128)S(1)} all-to-all(f32[16,1,128]{2,1,0:T(1,128)S(1)} %broadcast_in_dim.4), channel_id=1, replica_groups=mesh['zl'=4,'y'=8,'c'=2,'zh'=2,'x'=4] {'zl','zh','c'}, dimensions={0} | all-to-all | bytes 16384 | tf_op jit(solution)/shard_map/all_to_all | solution.py:377
  54.1 14.6 %all_to_all.13 = f32[32,1,128]{2,1,0:T(1,128)S(1)} all-to-all(f32[32,1,128]{2,1,0:T(1,128)S(1)} %broadcast_in_dim.5), channel_id=1, replica_groups=mesh['zl'=4,'y'=8,'c'=2,'zh'=2,'x'=4] {'y','x'}, dimensions={0} | all-to-all | bytes 32768 | tf_op jit(solution)/shard_map/all_to_all | solution.py:377
  68.7 0.5 slice_multiply_fusion
  (5 shorter events, 0.1 us)
Async XLA Ops:
  0.6 15.6 %copy-start = (f32[3,8,2,1024]{3,2,1,0:T(2,128)S(1)}, f32[3,8,2,1024]{3,2,1,0:T(2,128)}, u32[]{:S(2)}) copy-start(f32[3,8,2,1024]{3,2,1,0:T(2,128)} %param.7) | copy-start | bytes 589828
  0.6 15.6 %copy-start.1 = (f32[3,8,2,1024]{3,2,1,0:T(2,128)S(1)}, f32[3,8,2,1024]{3,2,1,0:T(2,128)}, u32[]{:S(2)}) copy-start(f32[3,8,2,1024]{3,2,1,0:T(2,128)} %param.9) | copy-start | bytes 589828
  0.7 15.6 %copy-start.2 = (f32[3,8,2,1024]{3,2,1,0:T(2,128)S(1)}, f32[3,8,2,1024]{3,2,1,0:T(2,128)}, u32[]{:S(2)}) copy-start(f32[3,8,2,1024]{3,2,1,0:T(2,128)} %param.8) | copy-start | bytes 589828
  0.7 15.6 %copy-start.3 = (f32[3,8,2,1024]{3,2,1,0:T(2,128)S(1)}, f32[3,8,2,1024]{3,2,1,0:T(2,128)}, u32[]{:S(2)}) copy-start(f32[3,8,2,1024]{3,2,1,0:T(2,128)} %param.10) | copy-start | bytes 589828
  0.7 15.6 %copy-start.4 = (s32[8,2,1024]{2,1,0:T(2,128)S(1)}, s32[8,2,1024]{2,1,0:T(2,128)}, u32[]{:S(2)}) copy-start(s32[8,2,1024]{2,1,0:T(2,128)} %param.11) | copy-start | bytes 196612
  3.2 27.7 %collective-permute-start = (f32[66,8,128]{2,1,0:T(8,128)}, f32[66,8,128]{2,1,0:T(8,128)S(1)}, u32[]{:S(2)}, u32[]{:S(2)}) collective-permute-start(f32[66,8,128]{2,1,0:T(8,128)} %get-tuple-element.18), channel_id=1, source_target_pairs={{1,2},{2,1},{3,4},{4,3},{5,6},{6,5},{9,10},{10,9},{11,12},{12,11},... | collective-permute-start | bytes 811016 | tf_op jit(solution)/shard_map/ppermute | solution.py:371
  3.9 12.4 %collective-permute-start.2 = (f32[13,2,16,128]{3,2,1,0:T(8,128)}, f32[13,2,16,128]{3,2,1,0:T(8,128)S(1)}, u32[]{:S(2)}, u32[]{:S(2)}) collective-permute-start(f32[13,2,16,128]{3,2,1,0:T(8,128)} %get-tuple-element.22), channel_id=1, source_target_pairs={{8,16},{16,8},{24,32},{32,24},{40,48},{48,40},{56,64},{64,56},{72,... | collective-permute-start | bytes 638984 | tf_op jit(solution)/shard_map/ppermute | solution.py:371
  8.5 7.9 %copy-start.6 = (f32[4]{0:T(128)S(1)}, f32[4]{0:T(128)}, u32[]{:S(2)}) copy-start(f32[4]{0:T(128)} %eps_ref.5) | copy-start | bytes 52
  8.5 7.8 %collective-permute-start.3 = (f32[13,2,16,128]{3,2,1,0:T(8,128)}, f32[13,2,16,128]{3,2,1,0:T(8,128)S(1)}, u32[]{:S(2)}, u32[]{:S(2)}) collective-permute-start(f32[13,2,16,128]{3,2,1,0:T(8,128)} %get-tuple-element.23), channel_id=1, source_target_pairs={{0,8},{8,0},{1,9},{9,1},{2,10},{10,2},{3,11},{11,3},{4,12},{12,4},... | collective-permute-start | bytes 638984 | tf_op jit(solution)/shard_map/ppermute | solution.py:371
  13.3 17.5 %collective-permute-start.1 = (f32[40,8,128]{2,1,0:T(8,128)}, f32[40,8,128]{2,1,0:T(8,128)S(1)}, u32[]{:S(2)}, u32[]{:S(2)}) collective-permute-start(f32[40,8,128]{2,1,0:T(8,128)} %get-tuple-element.19), channel_id=1, source_target_pairs={{0,1},{1,0},{2,3},{3,2},{4,5},{5,4},{6,7},{7,6},{8,9},{9,8},{10,11... | collective-permute-start | bytes 491528 | tf_op jit(solution)/shard_map/ppermute | solution.py:371
  17.3 13.6 %collective-permute-start.4 = (f32[21,8,128]{2,1,0:T(8,128)S(1)}, f32[21,8,128]{2,1,0:T(8,128)S(1)}, u32[]{:S(2)}, u32[]{:S(2)}) collective-permute-start(f32[21,8,128]{2,1,0:T(8,128)S(1)} %get-tuple-element.24), channel_id=1, source_target_pairs={{1,2},{2,1},{3,4},{4,3},{5,6},{6,5},{9,10},{10,9},{11,12},{12,11},... | collective-permute-start | bytes 258056 | tf_op jit(solution)/shard_map/ppermute | solution.py:371
  18.0 16.9 %copy-start.5 = (s32[8,2,1024]{2,1,0:T(2,128)S(1)}, s32[8,2,1024]{2,1,0:T(2,128)}, u32[]{:S(2)}) copy-start(s32[8,2,1024]{2,1,0:T(2,128)} %param.12) | copy-start | bytes 196612
  18.0 16.9 %collective-permute-start.5 = (f32[47,8,128]{2,1,0:T(8,128)S(1)}, f32[47,8,128]{2,1,0:T(8,128)S(1)}, u32[]{:S(2)}, u32[]{:S(2)}) collective-permute-start(f32[47,8,128]{2,1,0:T(8,128)S(1)} %get-tuple-element.25), channel_id=1, source_target_pairs={{0,1},{1,0},{2,3},{3,2},{4,5},{5,4},{6,7},{7,6},{8,9},{9,8},{10,11... | collective-permute-start | bytes 577544 | tf_op jit(solution)/shard_map/ppermute | solution.py:371

commit v7 on v6

--- a/solution.py
+++ b/solution.py
@@ -431,7 +431,7 @@
     )(early1, early0)
     out_e, out_h, sums = pl.pallas_call(
         final_kernel,
-        out_shape=(f32(3, 8, 16, 128), f32(3, 8, 16, 128), f32(1, 128)),
+        out_shape=(f32(3, 8, 16, 128), f32(3, 8, 16, 128), f32(lax.axis_size(("zl", "zh", "c")), 128)),
         in_specs=[SMEM] + [VMEM] * 12,
         out_specs=[HBM, HBM, VMEM],
         scratch_shapes=[
@@ -442,7 +442,7 @@
         compiler_params=PARAMS,
         name="final_step",
     )(permittivity, e, g, m, own, early1, early0, late1, late0, t1s, s1s, s0s, cs)
-    total = spread_sum(sums[0], ("zl", "zh", "c"))
+    total = jnp.sum(lax.all_to_all(sums, ("zl", "zh", "c"), 0, 0, tiled=True), axis=0)
     total = spread_sum(total, ("y", "x"))
     cells = 8 * lax.axis_size(XY) * 2 * lax.axis_size(GZ) * 1024
     gradient = total[:NI] / jnp.sqrt(jnp.float32(cells / NI))

time: 69.6 us -> 69.6 us (level)
    all_to_all x2 -> x1, blocking collectives: 31.8 us -> 14.6 us  [spread_sum(): return jnp.sum(lax.all_to_all(sent, axes, 0, 0), axis=0)]
    all_to_all x0 -> x1, blocking collectives: none -> 17.2 us  [body(): lax.all_to_all(sums, ('zl', 'zh', 'c'), 0, 0, tiled=True)]
where the time goes in v7:
time: 69.6 us; the launch traced here: 69.2 us
  blocking collectives  31.8 us (46%)
  starting transfers between devices  26.5 us (38%)
  Pallas kernels  5.34 us (8%)
  waiting for transfers between devices  4.06 us (6%)
  between operations  0.85 us (1%)
    ppermute x6, starting transfers between devices, swap_pairs(): return lax.ppermute(value, axes, pairs)  26.5 us
    all_to_all x1, blocking collectives, body(): lax.all_to_all(sums, ('zl', 'zh', 'c'), 0, 0, tiled=True)  17.2 us
    all_to_all x1, blocking collectives, spread_sum(): return jnp.sum(lax.all_to_all(sent, axes, 0, 0), axis=0)  14.6 us
    ppermute x6, waiting for transfers between devices, swap_pairs(): return lax.ppermute(value, axes, pairs)  4.06 us
    pallas_call x1, Pallas kernels, body(): pl.pallas_call(pack_kernel, out_shape=(f32(HALO, 2, 16, 128), f32(HALO, 2...  2.48 us
    pallas_call x1, Pallas kernels, body(): pl.pallas_call(final_kernel, out_shape=(f32(3, 8, 16, 128), f32(3, 8, 16,...  1.9 us
  transfers between devices with their start and end apart: 6, of which 1 were waited for; matrix products, arithmetic and copies ran while one was open for 0% of the time, Pallas kernels for 1%

profile of v7, /device:TPU:1, one launch (start us, length us, event | category | flops | bytes accessed | tf_op | source)
XLA Modules:
  0.0 69.2 jit_solution(1095683777468095435)
XLA Ops:
  0.6 0.0 copy-start
  0.6 0.0 copy-start.1
  0.7 0.0 copy-start.2
  0.7 0.0 copy-start.3
  0.7 0.0 copy-start.4
  0.7 2.5 %pack.1 = (f32[13,2,16,128]{3,2,1,0:T(8,128)}, f32[13,2,16,128]{3,2,1,0:T(8,128)}, f32[40,8,128]{2,1,0:T(8,128)}, f32[66,8,128]{2,1,0:T(8,128)}) custom-call(f32[4]{0:T(128)} %eps_ref.5, f32[3,8,16,128]{3,2,1,0:T(8,128)} %bitcast.44, f32[3,8,16,128]{3,2,1,0:T(8,128)} %bitcast.50, f32[3,8,16,128]{3,2,1,0:T(8,128)} %bitcast.47, f32[3,8,16,128]{3,2,1,0:T(8,128)} %bitcast.52, ...), custom_call_target="tpu_custom_call" | custom-call | tf_op jit(solution)/shard_map/pack/pallas_call | solution.py:382
  3.2 0.7 collective-permute-start
  3.9 4.6 %collective-permute-start.2 = (f32[13,2,16,128]{3,2,1,0:T(8,128)}, f32[13,2,16,128]{3,2,1,0:T(8,128)S(1)}, u32[]{:S(2)}, u32[]{:S(2)}) collective-permute-start(f32[13,2,16,128]{3,2,1,0:T(8,128)} %get-tuple-element.22), channel_id=1, source_target_pairs={{8,16},{16,8},{24,32},{32,24},{40,48},{48,40},{56,64},{64,56},{72,... | collective-permute-start | bytes 638984 | tf_op jit(solution)/shard_map/ppermute | solution.py:371
  8.5 0.0 copy-start.6
  8.5 4.9 %collective-permute-start.3 = (f32[13,2,16,128]{3,2,1,0:T(8,128)}, f32[13,2,16,128]{3,2,1,0:T(8,128)S(1)}, u32[]{:S(2)}, u32[]{:S(2)}) collective-permute-start(f32[13,2,16,128]{3,2,1,0:T(8,128)} %get-tuple-element.23), channel_id=1, source_target_pairs={{0,8},{8,0},{1,9},{9,1},{2,10},{10,2},{3,11},{11,3},{4,12},{12,4},... | collective-permute-start | bytes 638984 | tf_op jit(solution)/shard_map/ppermute | solution.py:371
  13.3 2.9 %collective-permute-start.1 = (f32[40,8,128]{2,1,0:T(8,128)}, f32[40,8,128]{2,1,0:T(8,128)S(1)}, u32[]{:S(2)}, u32[]{:S(2)}) collective-permute-start(f32[40,8,128]{2,1,0:T(8,128)} %get-tuple-element.19), channel_id=1, source_target_pairs={{0,1},{1,0},{2,3},{3,2},{4,5},{5,4},{6,7},{7,6},{8,9},{9,8},{10,11... | collective-permute-start | bytes 491528 | tf_op jit(solution)/shard_map/ppermute | solution.py:371
  16.2 0.0 collective-permute-done.2.next_ref
  16.3 0.0 collective-permute-done.3.pair_ref
  16.3 0.0 copy-done
  16.3 0.0 copy-done.1
  16.3 0.0 copy-done.2
  16.3 0.0 copy-done.3
  16.3 0.0 copy-done.4
  16.3 0.0 copy-done.6
  16.3 1.0 %local_step.1 = (f32[47,8,128]{2,1,0:T(8,128)S(1)}, f32[21,8,128]{2,1,0:T(8,128)S(1)}, f32[2,3,2,11,8,128]{5,4,3,2,1,0:T(8,128)S(1)}, f32[2,3,2,10,8,128]{5,4,3,...) custom-call(f32[4]{0:T(128)S(1)} %copy-done.6, f32[3,8,16,128]{3,2,1,0:T(8,128)S(1)} %bitcast.45, ...), custom_call_target="tpu_custom_call" | custom-call | flops 1 | bytes 1 | tf_op jit(solution)/shard_map/local_step/pallas_call | solution.py:404
  17.3 0.7 collective-permute-start.4
  18.0 0.0 copy-start.5
  18.0 12.8 %collective-permute-start.5 = (f32[47,8,128]{2,1,0:T(8,128)S(1)}, f32[47,8,128]{2,1,0:T(8,128)S(1)}, u32[]{:S(2)}, u32[]{:S(2)}) collective-permute-start(f32[47,8,128]{2,1,0:T(8,128)S(1)} %get-tuple-element.25), channel_id=1, source_target_pairs={{0,1},{1,0},{2,3},{3,2},{4,5},{5,4},{6,7},{7,6},{8,9},{9,8},{10,11... | collective-permute-start | bytes 577544 | tf_op jit(solution)/shard_map/ppermute | solution.py:371
  30.8 0.0 collective-permute-done.1.refs_1_
  30.8 0.0 collective-permute-done.refs_0_
  30.9 0.0 collective-permute-done.4.late1
  30.9 4.0 %collective-permute-done.5.late0 = f32[47,8,128]{2,1,0:T(8,128)S(1)} collective-permute-done((f32[47,8,128]{2,1,0:T(8,128)S(1)}, f32[47,8,128]{2,1,0:T(8,128)S(1)}, u32[]{:S(2)}, u32[]{:S(2)}) %collective-permute-start.5) | collective-permute-done | bytes 192544 | tf_op jit(solution)/shard_map/ppermute | solution.py:371
  34.9 0.0 copy-done.5
  34.9 1.9 %final_step.1 = (f32[3,8,16,128]{3,2,1,0:T(8,128)}, f32[3,8,16,128]{3,2,1,0:T(8,128)}, f32[16,128]{1,0:T(8,128)S(1)}) custom-call(f32[4]{0:T(128)S(1)} %copy-done.6, f32[3,8,16,128]{3,2,1,0:T(8,128)S(1)} %bitcast.46, f32[3,8,16,128]{3,2,1,0:T(8,128)S(1)} %bitcast.49, s32[8,16,128]{2,1,0:T(8,128)S(1)} %bitcast.56, s32[8,16,128]{2,1,0:T(8,128)S(1)} %bitcast.57, ...), custom_call_target="tpu_custom_call" | custom-call | tf_op jit(solution)/shard_map/final_step/pallas_call | solution.py:432
  36.8 17.2 %all_to_all.15 = f32[16,1,128]{2,1,0:T(1,128)S(1)} all-to-all(f32[16,1,128]{2,1,0:T(1,128)S(1)} %bitcast.58), channel_id=1, replica_groups=mesh['zl'=4,'y'=8,'c'=2,'zh'=2,'x'=4] {'zl','zh','c'}, dimensions={0} | all-to-all | bytes 16384 | tf_op jit(solution)/shard_map/all_to_all | solution.py:445
  54.1 14.6 %all_to_all.16 = f32[32,1,128]{2,1,0:T(1,128)S(1)} all-to-all(f32[32,1,128]{2,1,0:T(1,128)S(1)} %broadcast_in_dim.2), channel_id=1, replica_groups=mesh['zl'=4,'y'=8,'c'=2,'zh'=2,'x'=4] {'y','x'}, dimensions={0} | all-to-all | bytes 32768 | tf_op jit(solution)/shard_map/all_to_all | solution.py:377
  68.7 0.5 slice_multiply_fusion
  (4 shorter events, 0.1 us)
Async XLA Ops:
  0.6 15.6 %copy-start = (f32[3,8,2,1024]{3,2,1,0:T(2,128)S(1)}, f32[3,8,2,1024]{3,2,1,0:T(2,128)}, u32[]{:S(2)}) copy-start(f32[3,8,2,1024]{3,2,1,0:T(2,128)} %param.7) | copy-start | bytes 589828
  0.6 15.6 %copy-start.1 = (f32[3,8,2,1024]{3,2,1,0:T(2,128)S(1)}, f32[3,8,2,1024]{3,2,1,0:T(2,128)}, u32[]{:S(2)}) copy-start(f32[3,8,2,1024]{3,2,1,0:T(2,128)} %param.9) | copy-start | bytes 589828
  0.7 15.6 %copy-start.2 = (f32[3,8,2,1024]{3,2,1,0:T(2,128)S(1)}, f32[3,8,2,1024]{3,2,1,0:T(2,128)}, u32[]{:S(2)}) copy-start(f32[3,8,2,1024]{3,2,1,0:T(2,128)} %param.8) | copy-start | bytes 589828
  0.7 15.6 %copy-start.3 = (f32[3,8,2,1024]{3,2,1,0:T(2,128)S(1)}, f32[3,8,2,1024]{3,2,1,0:T(2,128)}, u32[]{:S(2)}) copy-start(f32[3,8,2,1024]{3,2,1,0:T(2,128)} %param.10) | copy-start | bytes 589828
  0.7 15.6 %copy-start.4 = (s32[8,2,1024]{2,1,0:T(2,128)S(1)}, s32[8,2,1024]{2,1,0:T(2,128)}, u32[]{:S(2)}) copy-start(s32[8,2,1024]{2,1,0:T(2,128)} %param.11) | copy-start | bytes 196612
  3.2 27.7 %collective-permute-start = (f32[66,8,128]{2,1,0:T(8,128)}, f32[66,8,128]{2,1,0:T(8,128)S(1)}, u32[]{:S(2)}, u32[]{:S(2)}) collective-permute-start(f32[66,8,128]{2,1,0:T(8,128)} %get-tuple-element.18), channel_id=1, source_target_pairs={{1,2},{2,1},{3,4},{4,3},{5,6},{6,5},{9,10},{10,9},{11,12},{12,11},... | collective-permute-start | bytes 811016 | tf_op jit(solution)/shard_map/ppermute | solution.py:371
  3.9 12.4 %collective-permute-start.2 = (f32[13,2,16,128]{3,2,1,0:T(8,128)}, f32[13,2,16,128]{3,2,1,0:T(8,128)S(1)}, u32[]{:S(2)}, u32[]{:S(2)}) collective-permute-start(f32[13,2,16,128]{3,2,1,0:T(8,128)} %get-tuple-element.22), channel_id=1, source_target_pairs={{8,16},{16,8},{24,32},{32,24},{40,48},{48,40},{56,64},{64,56},{72,... | collective-permute-start | bytes 638984 | tf_op jit(solution)/shard_map/ppermute | solution.py:371
  8.5 7.9 %copy-start.6 = (f32[4]{0:T(128)S(1)}, f32[4]{0:T(128)}, u32[]{:S(2)}) copy-start(f32[4]{0:T(128)} %eps_ref.5) | copy-start | bytes 52
  8.5 7.8 %collective-permute-start.3 = (f32[13,2,16,128]{3,2,1,0:T(8,128)}, f32[13,2,16,128]{3,2,1,0:T(8,128)S(1)}, u32[]{:S(2)}, u32[]{:S(2)}) collective-permute-start(f32[13,2,16,128]{3,2,1,0:T(8,128)} %get-tuple-element.23), channel_id=1, source_target_pairs={{0,8},{8,0},{1,9},{9,1},{2,10},{10,2},{3,11},{11,3},{4,12},{12,4},... | collective-permute-start | bytes 638984 | tf_op jit(solution)/shard_map/ppermute | solution.py:371
  13.3 17.5 %collective-permute-start.1 = (f32[40,8,128]{2,1,0:T(8,128)}, f32[40,8,128]{2,1,0:T(8,128)S(1)}, u32[]{:S(2)}, u32[]{:S(2)}) collective-permute-start(f32[40,8,128]{2,1,0:T(8,128)} %get-tuple-element.19), channel_id=1, source_target_pairs={{0,1},{1,0},{2,3},{3,2},{4,5},{5,4},{6,7},{7,6},{8,9},{9,8},{10,11... | collective-permute-start | bytes 491528 | tf_op jit(solution)/shard_map/ppermute | solution.py:371
  17.3 13.6 %collective-permute-start.4 = (f32[21,8,128]{2,1,0:T(8,128)S(1)}, f32[21,8,128]{2,1,0:T(8,128)S(1)}, u32[]{:S(2)}, u32[]{:S(2)}) collective-permute-start(f32[21,8,128]{2,1,0:T(8,128)S(1)} %get-tuple-element.24), channel_id=1, source_target_pairs={{1,2},{2,1},{3,4},{4,3},{5,6},{6,5},{9,10},{10,9},{11,12},{12,11},... | collective-permute-start | bytes 258056 | tf_op jit(solution)/shard_map/ppermute | solution.py:371
  18.0 16.9 %copy-start.5 = (s32[8,2,1024]{2,1,0:T(2,128)S(1)}, s32[8,2,1024]{2,1,0:T(2,128)}, u32[]{:S(2)}) copy-start(s32[8,2,1024]{2,1,0:T(2,128)} %param.12) | copy-start | bytes 196612
  18.0 16.9 %collective-permute-start.5 = (f32[47,8,128]{2,1,0:T(8,128)S(1)}, f32[47,8,128]{2,1,0:T(8,128)S(1)}, u32[]{:S(2)}, u32[]{:S(2)}) collective-permute-start(f32[47,8,128]{2,1,0:T(8,128)S(1)} %get-tuple-element.25), channel_id=1, source_target_pairs={{0,1},{1,0},{2,3},{3,2},{4,5},{5,4},{6,7},{7,6},{8,9},{9,8},{10,11... | collective-permute-start | bytes 577544 | tf_op jit(solution)/shard_map/ppermute | solution.py:371
